TPU v7x, 256 devices: a whole 4x4x8 slice. The times are simulated.
256 devices in a mesh: dp: 64 (over z, y, core), feat: 4 (over x).
Axes of the slice: x: 4, y: 4, z: 8, core: 2. Of those that a mesh axis runs over, the one named last changes fastest.
Arguments:
- embeddings: bfloat16 [65536, 512], P('dp', 'feat'), may hold values from -6 to 6
- code_ids: int32 [3, 65536], P(None, 'dp'), may hold values from 0 to 8191, as said below
- codebooks: float32 [3, 8192, 512], P(None, 'dp', 'feat'), may hold values from -4 to 4
- item_weight: bfloat16 [65536], P('dp'), may hold values from 0.25 to 4
Outputs:
- updated_books: float32 [3, 8192, 512], P(None, 'dp', 'feat')
- final_residual: bfloat16 [65536, 512], P('dp', 'feat')
- item_error: float32 [65536], P('dp')
Inputs may be any that keep to these rules, and one draw needn't show every extreme that they name: `code_ids`: codes k with o * 128 <= k < (o + 1) * 128 form run o. In each section, each aligned block of 1024 items holds at most 32 items whose codes lie in one run, and in every section some run receives exactly 32 items from every block.
All inputs are finite; a program needn't handle non-finite values.
Results may differ from a plain program's by a relative error of at most 0.0057.
Values may be sent and summed in bfloat16 or wider, within the bound.
No kernel may reach another device: no remote copies, remote signals or barrier semaphores. Data moves between devices by JAX's collectives and lax.ppermute only.
A program may use at most 64 MiB of HBM per device.

v0:
```python
import jax
import jax.numpy as jnp
from jax import lax
from jax.sharding import PartitionSpec as P

CODES = 8192
SECTIONS = 3


prior_weight = 4.0


def per_device(embeddings, code_ids, codebooks, item_weight):
    residual = embeddings
    own_codes = codebooks.shape[1]
    weights_wide = item_weight.astype(jnp.float32)
    updated_all = []
    counts_local = jnp.stack(
        [
            jax.ops.segment_sum(weights_wide, code_ids[section_idx], num_segments=CODES)
            for section_idx in range(SECTIONS)
        ]
    )
    counts_owned = lax.psum_scatter(counts_local, "dp", scatter_dimension=1, tiled=True)
    for section_idx in range(SECTIONS):
        codes_now = code_ids[section_idx]
        targets = jnp.arange(lax.axis_size("dp") * own_codes, dtype=jnp.int32)
        onehot = (codes_now[:, None] == targets[None, :]).astype(jnp.bfloat16) * item_weight[
            :, None
        ]
        code_sums = lax.psum_scatter(
            lax.dot_general(
                onehot, residual, (((0,), (0,)), ((), ())), preferred_element_type=jnp.float32
            ),
            "dp",
            scatter_dimension=0,
            tiled=True,
        )
        updated = (prior_weight * codebooks[section_idx] + code_sums) / (
            prior_weight + counts_owned[section_idx]
        )[:, None]
        gathered = lax.all_gather(updated, "dp", axis=0, tiled=True)
        centroid_rows = jnp.take(gathered, codes_now, axis=0)
        updated_all.append(updated)
        residual = (residual.astype(jnp.float32) - centroid_rows).astype(jnp.bfloat16)
    wide = residual.astype(jnp.float32)
    item_error = lax.psum(jnp.sum(wide * wide, axis=1), "feat")
    return (jnp.stack(updated_all), residual, item_error)


def solution(mesh):
    in_specs = (P("dp", "feat"), P(None, "dp"), P(None, "dp", "feat"), P("dp"))
    out_specs = (P(None, "dp", "feat"), P("dp", "feat"), P("dp"))
    return jax.shard_map(
        per_device, mesh=mesh, in_specs=in_specs, out_specs=out_specs, check_vma=False
    )
```

profile of v0, /device:TPU:8, one launch (start us, length us, event | category | flops | bytes accessed | tf_op | source)
XLA Modules:
  0.0 895.0 jit_solution(698870047051932519)
XLA Ops:
  7.2 0.7 convert_element_type.27
  7.9 0.8 fusion.37
  8.7 5.9 scatter_custom_fusion
  14.7 5.9 scatter_custom_fusion.1
  20.6 5.9 scatter_custom_fusion.2
  26.6 0.1 pad_maximum_fusion.1
  26.7 2.7 copy.7
  29.5 7.2 fusion.7
  36.7 138.6 %reduce-scatter.13.cloned.1.call-done = f32[128,3]{1,0:T(8,128)} async-done(((f32[8192,3]{1,0:T(8,128)}), f32[128,3]{1,0:T(8,128)}) %reduce-scatter.13.cloned.1.call-update) | async-done | bytes 1552
  175.4 1.0 slice_add_fusion
  176.4 0.1 copy.12
  176.5 145.8 %reduce-scatter.7.cloned.1.call-done = f32[128,128]{1,0:T(8,128)} async-done(((f32[8192,128]{1,0:T(8,128)}), f32[128,128]{1,0:T(8,128)}) %reduce-scatter.7.cloned.1.call-update) | async-done | bytes 65552 | tf_op jit(solution)/shard_map/reduce_scatter | solution.py:31
  322.3 1.6 fusion.23
  323.9 0.2 reduce-scatter.9.cloned.1.call-start
  324.2 78.6 %all-gather.4.cloned.1.call-done = f32[8192,128]{1,0:T(8,128)} async-done(((f32[128,128]{1,0:T(8,128)}), f32[8192,128]{1,0:T(8,128)}) %all-gather.4.cloned.1.call-update) | async-done | bytes 4194320 | tf_op jit(solution)/shard_map/all_gather | solution.py:42
  402.8 5.0 gather_fusion
  407.8 0.2 fusion.20
  408.0 7.2 fusion.5
  415.3 141.4 %reduce-scatter.9.cloned.1.call-done = f32[128,128]{1,0:T(8,128)} async-done(((f32[8192,128]{1,0:T(8,128)}), f32[128,128]{1,0:T(8,128)}) %reduce-scatter.9.cloned.1.call-update) | async-done | bytes 65552 | tf_op jit(solution)/shard_map/reduce_scatter | solution.py:31
  556.7 1.6 fusion.22
  558.4 79.1 %all-gather.6.cloned.1.call-done = f32[8192,128]{1,0:T(8,128)} async-done(((f32[128,128]{1,0:T(8,128)}), f32[8192,128]{1,0:T(8,128)}) %all-gather.6.cloned.1.call-update) | async-done | bytes 4194320 | tf_op jit(solution)/shard_map/all_gather | solution.py:42
  637.4 5.0 gather_fusion.1
  642.4 0.2 fusion.19
  642.6 7.2 fusion.3
  649.9 0.1 copy.14
  649.9 141.5 %reduce-scatter.11.cloned.1.call-done = f32[128,128]{1,0:T(8,128)} async-done(((f32[8192,128]{1,0:T(8,128)}), f32[128,128]{1,0:T(8,128)}) %reduce-scatter.11.cloned.1.call-update) | async-done | bytes 65552 | tf_op jit(solution)/shard_map/reduce_scatter | solution.py:31
  791.4 1.6 fusion.21
  793.0 1.5 pad_maximum_fusion
  794.6 76.7 %all-gather.8.cloned.1.call-done = f32[8192,128]{1,0:T(8,128)} async-done(((f32[128,128]{1,0:T(8,128)}), f32[8192,128]{1,0:T(8,128)}) %all-gather.8.cloned.1.call-update) | async-done | bytes 4194320 | tf_op jit(solution)/shard_map/all_gather | solution.py:42
  871.3 5.0 gather_fusion.2
  876.2 0.9 multiply_reduce_fusion
  877.2 11.0 %psum.7 = f32[1024]{0:T(1024)} all-reduce(f32[1024]{0:T(1024)S(1)} %get-tuple-element.4), channel_id=1, replica_groups=mesh['dp'=64,'feat'=4] {'feat'}, use_global_device_ids=true, to_apply=%region_8.10 | all-reduce | flops 1024 | bytes 8192 | tf_op jit(solution)/shard_map/psum | solution.py:47
  (30 shorter events, 0.5 us)
Async XLA Ops:
  7.2 168.2 %reduce-scatter.13.cloned.1.call-start = ((), (), s32[]{:S(2)}) async-start(), calls=%async_computation.10 | async-start | bytes 4259840
  26.7 2.8 copy-start.2
  26.7 2.8 copy-start.4
  29.4 292.9 %reduce-scatter.7.cloned.1.call-start = ((), (), s32[]{:S(2)}) async-start(), calls=%async_computation.4 | async-start | bytes 4259840 | tf_op jit(solution)/shard_map/reduce_scatter | solution.py:31
  36.7 285.7 %copy-start.3 = (f32[3,128,128]{2,1,0:T(8,128)S(1)}, f32[3,128,128]{2,1,0:T(8,128)}, u32[]{:S(2)}) copy-start(f32[3,128,128]{2,1,0:T(8,128)} %param.8) | copy-start | bytes 589828
  36.7 366.1 %all-gather.4.cloned.1.call-start = ((), (), s32[]{:S(2)}) async-start(), calls=%async_computation.5 | async-start | bytes 4259840 | tf_op jit(solution)/shard_map/all_gather | solution.py:42
  323.9 232.8 %reduce-scatter.9.cloned.1.call-start = ((), (), s32[]{:S(2)}) async-start(), calls=%async_computation.6 | async-start | bytes 4259840 | tf_op jit(solution)/shard_map/reduce_scatter | solution.py:31
  415.2 222.2 %all-gather.6.cloned.1.call-start = ((), (), s32[]{:S(2)}) async-start(), calls=%async_computation.7 | async-start | bytes 4259840 | tf_op jit(solution)/shard_map/all_gather | solution.py:42
  558.3 233.1 %reduce-scatter.11.cloned.1.call-start = ((), (), s32[]{:S(2)}) async-start(), calls=%async_computation.8 | async-start | bytes 4259840 | tf_op jit(solution)/shard_map/reduce_scatter | solution.py:31
  649.8 143.2 %copy-start = (f32[128,128]{1,0:T(8,128)S(1)}, f32[128,128]{1,0:T(8,128)}, u32[]{:S(2)}) copy-start(f32[128,128]{1,0:T(8,128)} %fusion.23) | copy-start | bytes 196612
  649.8 143.3 %copy-start.1 = (f32[128,128]{1,0:T(8,128)S(1)}, f32[128,128]{1,0:T(8,128)}, u32[]{:S(2)}) copy-start(f32[128,128]{1,0:T(8,128)} %fusion.22) | copy-start | bytes 196612
  649.8 221.4 %all-gather.8.cloned.1.call-start = ((), (), s32[]{:S(2)}) async-start(), calls=%async_computation.9 | async-start | bytes 4259840 | tf_op jit(solution)/shard_map/all_gather | solution.py:42
Sparse Core Ops, SparseCore 0:
  29.5 145.7 reduce-scatter.12
  180.1 142.1 reduce-scatter.6
  325.7 77.0 all-gather.3
  415.3 141.3 reduce-scatter.8
  560.3 77.0 all-gather.5
  649.9 141.4 reduce-scatter.10
  794.2 77.0 all-gather.7
where the time goes:
time: 896 us; the launch traced here: 895 us
  waiting for transfers between devices  802 us (90%)
  other arithmetic  27.2 us (3%)
  matrix products  21.5 us (2%)
  local copies, waits for them, and re-layouts  18.7 us (2%)
  between operations  14.3 us (2%)
  blocking collectives  11 us (1%)
    reduce_scatter x3, waiting for transfers between devices, per_device(): lax.psum_scatter(lax.dot_general(onehot, residual, (((0,), (0,)), ((), ()...  429 us
    all_gather x3, waiting for transfers between devices, per_device(): gathered = lax.all_gather(updated, 'dp', axis=0, tiled=True)  234 us
    unnamed x8, waiting for transfers between devices  139 us
    dot_general x3, matrix products, per_device(): lax.dot_general(onehot, residual, (((0,), (0,)), ((), ())), preferred_ele...  21.5 us
  transfers between devices with their start and end apart: 7, of which 7 were waited for; matrix products, arithmetic and copies ran while one was open for 1% of the time, Pallas kernels for 0%

commit v1 on v0

v1 whole, which is shorter than its diff:
```python
import jax
import jax.numpy as jnp
from jax import lax
from jax.experimental import pallas as pl
from jax.experimental.pallas import tpu as pltpu
from jax.sharding import PartitionSpec as P

F32 = jnp.float32
BF16 = jnp.bfloat16
SECTIONS = 3
RUNS = 64
BLOCKS = 64
FEATS = 128
prior_weight = 4.0

ROWS_IN = 64
ROWS_OUT = 32


def two_parts(x):
    head = x.astype(BF16).astype(F32)
    return head, x - head


def pack_kernel(emb_ref, ids_ref, w_ref, book_ref, out_ref, emb_rows, book_rows):
    for block in range(8):
        turned = emb_ref[block * 128 : (block + 1) * 128, :].astype(F32).T
        for group in range(16):
            which, first = group // 8, (group % 8) * 8
            emb_rows[pl.ds(first * 16 + which * 8 + block, 8, stride=16), :] = turned[
                group * 8 : (group + 1) * 8
            ]
    book_rows[...] = jnp.zeros_like(book_rows)
    for section in range(SECTIONS):
        parts = two_parts(book_ref[section].T)
        for part in range(2):
            for group in range(16):
                which, first = group // 8, (group % 8) * 8
                book_rows[
                    pl.ds(first * 16 + part * 8 + section * 2 + which, 8, stride=16), :
                ] = parts[part][group * 8 : (group + 1) * 8]
    ids = ids_ref[...]
    run = ids >> 7
    coded = ((ids & 127) + 128).astype(F32)
    for bit in range(6):
        coded = coded * jnp.where((run >> bit) & 1 == 1, 2.0 ** (1 << bit), 1.0)
    shared = jnp.concatenate([coded, w_ref[...].astype(F32)], axis=0).astype(BF16)

    @pl.loop(0, RUNS)
    def _(dest):
        out_ref[dest, 0:16, :] = emb_rows[pl.ds(pl.multiple_of(dest * 16, 16), 16), :].astype(BF16)
        out_ref[dest, 16:48, :] = shared
        out_ref[dest, 48:64, :] = book_rows[pl.ds(pl.multiple_of(dest * 16, 16), 16), :].astype(
            BF16
        )


def wide_row(ref, row, size):
    return jnp.broadcast_to(ref[pl.ds(row, 1), :], (size, 128))


def sections_kernel(
    in_ref, out_ref, runs, codes, weights, residual, books_in, books_out, table, total
):
    @pl.loop(0, BLOCKS)
    def _(block):
        at = pl.ds(pl.multiple_of(block * 8, 8), 8)
        values = in_ref[block, 0:16, :].astype(F32)
        residual[0, at, :] = values[0:8]
        residual[1, at, :] = values[8:16]
        shared = in_ref[block, 16:48, :].astype(F32)
        weights[at, :] = shared[24:32]
        coded = shared[0:24]
        run = jnp.zeros_like(coded)
        for bit in range(5, -1, -1):
            over = coded >= 128.0 * 2.0 ** (1 << bit)
            coded = jnp.where(over, coded * 2.0 ** -(1 << bit), coded)
            run = run + jnp.where(over, float(1 << bit), 0.0)
        for section in range(SECTIONS):
            runs[section, at, :] = run[section * 8 : section * 8 + 8]
            codes[section, at, :] = coded[section * 8 : section * 8 + 8] - 128.0
        books_in[pl.ds(pl.multiple_of(block * 16, 16), 16), :] = in_ref[block, 48:64, :].astype(F32)

    books_out[...] = jnp.zeros_like(books_out)
    down = lax.broadcasted_iota(jnp.int32, (16, 128), 0).astype(F32)
    iotas = [(down + 16.0 * step).astype(BF16) for step in range(8)]
    nought = jnp.zeros((16, 128), BF16)
    one = jnp.ones((16, 128), BF16)

    def add_block(section, block):
        lefts, rights = [], []
        for row in range(8):
            at = block * 8 + row
            run = wide_row(runs.at[section], at, 16).astype(BF16)
            code = wide_row(codes.at[section], at, 16).astype(BF16)
            weight = wide_row(weights, at, 16).astype(BF16)
            first = wide_row(residual.at[0], at, 16).astype(BF16)
            second = wide_row(residual.at[1], at, 16).astype(BF16)
            masks = [run == iotas[step] for step in range(4)]
            lefts.append(
                jnp.concatenate(
                    [
                        jnp.where(mask, value, nought)
                        for value in (first, second, one)
                        for mask in masks
                    ],
                    axis=0,
                )
            )
            rights.append(
                jnp.concatenate(
                    [jnp.where(code == iotas[step], weight, nought) for step in range(8)], axis=0
                )
            )
        total[...] += lax.dot_general(
            jnp.concatenate(lefts, axis=1),
            jnp.concatenate(rights, axis=1),
            (((1,), (1,)), ((), ())),
            preferred_element_type=F32,
        )

    def take_block(section, block):
        at = pl.ds(pl.multiple_of(block * 8, 8), 8)
        run = runs[section, at, :]
        code = codes[section, at, :].astype(jnp.int32)
        rows = [jnp.zeros((8, 128), F32)] * 2
        for each in range(RUNS):
            mask = run == float(each)
            for which in range(2):
                wide = wide_row(table.at[which], each, 8)
                found = jnp.take_along_axis(wide, code, axis=1)
                rows[which] = jnp.where(mask, found, rows[which])
        result = []
        for which in range(2):
            left = (residual[which, at, :] - rows[which]).astype(BF16)
            residual[which, at, :] = left.astype(F32)
            result.append(left)
        return result

    def update(section):
        count = prior_weight + total[128:192, :]
        for which in range(2):
            book = jnp.concatenate(
                [
                    books_in[pl.ds(first * 16 + section * 2 + which, 8, stride=16), :]
                    + books_in[pl.ds(first * 16 + 8 + section * 2 + which, 8, stride=16), :]
                    for first in range(0, RUNS, 8)
                ],
                axis=0,
            )
            new = (prior_weight * book + total[which * 64 : which * 64 + 64, :]) / count
            table[which] = new
            parts = two_parts(new)
            for part in range(2):
                for first in range(0, RUNS, 8):
                    books_out[
                        pl.ds(first * 16 + part * 8 + section * 2 + which, 8, stride=16), :
                    ] = parts[part][first : first + 8]
        total[...] = jnp.zeros_like(total)

    total[...] = jnp.zeros_like(total)

    @pl.loop(0, BLOCKS)
    def _(block):
        add_block(0, block)

    update(0)
    for section in range(1, SECTIONS):

        @pl.loop(0, BLOCKS)
        def _(block):
            take_block(section - 1, block)
            add_block(section, block)

        update(section)

    @pl.loop(0, BLOCKS)
    def _(block):
        left = take_block(SECTIONS - 1, block)
        out_ref[block, 0:16, :] = jnp.concatenate(left, axis=0)
        out_ref[block, 16:32, :] = books_out[
            pl.ds(pl.multiple_of(block * 16, 16), 16), :
        ].astype(BF16)


def unpack_kernel(in_ref, book_ref, left_ref, error_ref, left_rows, book_rows):
    def one(source, error):
        rows = in_ref[source, 0:16, :].astype(F32)
        at = pl.ds(pl.multiple_of(source * 16, 16), 16)
        left_rows[at, :] = rows
        book_rows[at, :] = in_ref[source, 16:32, :].astype(F32)
        return error + rows[0:8] * rows[0:8] + rows[8:16] * rows[8:16]

    error_ref[...] = lax.fori_loop(0, RUNS, one, jnp.zeros((8, 128), F32))
    for block in range(8):
        turned = jnp.concatenate(
            [
                left_rows[pl.ds(first * 16 + which * 8 + block, 8, stride=16), :]
                for which in range(2)
                for first in range(0, RUNS, 8)
            ],
            axis=0,
        )
        left_ref[block * 128 : (block + 1) * 128, :] = turned.T.astype(BF16)
    for section in range(SECTIONS):
        turned = jnp.concatenate(
            [
                book_rows[pl.ds(first * 16 + section * 2 + which, 8, stride=16), :]
                + book_rows[pl.ds(first * 16 + 8 + section * 2 + which, 8, stride=16), :]
                for which in range(2)
                for first in range(0, RUNS, 8)
            ],
            axis=0,
        )
        book_ref[section] = turned.T


def per_device(embeddings, code_ids, codebooks, item_weight):
    params = pltpu.CompilerParams(vmem_limit_bytes=48 * 1024 * 1024)
    with jax.named_scope("pack"):
        packed = pl.pallas_call(
            pack_kernel,
            out_shape=jax.ShapeDtypeStruct((RUNS, ROWS_IN, 128), BF16),
            scratch_shapes=[
                pltpu.VMEM((RUNS * 16, 128), F32),
                pltpu.VMEM((RUNS * 16, 128), F32),
            ],
            compiler_params=params,
        )(embeddings, code_ids.reshape(24, 128), item_weight.reshape(8, 128), codebooks)
    with jax.named_scope("to_features"):
        mine = lax.all_to_all(packed, "dp", 0, 0, tiled=True)
    with jax.named_scope("sections"):
        done = pl.pallas_call(
            sections_kernel,
            out_shape=jax.ShapeDtypeStruct((BLOCKS, ROWS_OUT, 128), BF16),
            scratch_shapes=[
                pltpu.VMEM((SECTIONS, BLOCKS * 8, 128), F32),
                pltpu.VMEM((SECTIONS, BLOCKS * 8, 128), F32),
                pltpu.VMEM((BLOCKS * 8, 128), F32),
                pltpu.VMEM((2, BLOCKS * 8, 128), F32),
                pltpu.VMEM((RUNS * 16, 128), F32),
                pltpu.VMEM((RUNS * 16, 128), F32),
                pltpu.VMEM((2, RUNS, 128), F32),
                pltpu.VMEM((3 * RUNS, 128), F32),
            ],
            compiler_params=params,
        )(mine)
    with jax.named_scope("to_items"):
        back = lax.all_to_all(done, "dp", 0, 0, tiled=True)
    with jax.named_scope("unpack"):
        updated, left, error = pl.pallas_call(
            unpack_kernel,
            out_shape=(
                jax.ShapeDtypeStruct((SECTIONS, 128, FEATS), F32),
                jax.ShapeDtypeStruct((1024, FEATS), BF16),
                jax.ShapeDtypeStruct((8, 128), F32),
            ),
            scratch_shapes=[
                pltpu.VMEM((RUNS * 16, 128), F32),
                pltpu.VMEM((RUNS * 16, 128), F32),
            ],
            compiler_params=params,
        )(back)
    with jax.named_scope("error"):
        item_error = lax.psum(error, "feat").reshape(1024)
    return updated, left, item_error


def solution(mesh):
    in_specs = (P("dp", "feat"), P(None, "dp"), P(None, "dp", "feat"), P("dp"))
    out_specs = (P(None, "dp", "feat"), P("dp", "feat"), P("dp"))
    return jax.shard_map(
        per_device, mesh=mesh, in_specs=in_specs, out_specs=out_specs, check_vma=False
    )
```

time: 896 us -> 169 us (0.19)
  waiting for transfers between devices: 802 us -> 0 us
  Pallas kernels: 0 us -> 91 us
  blocking collectives: 11 us -> 74.8 us
  other arithmetic: 27.2 us -> 0 us
  matrix products: 21.5 us -> 0 us
  local copies, waits for them, and re-layouts: 18.7 us -> 2.61 us
  between operations: 14.3 us -> 0.67 us
    reduce_scatter x3 -> x0, waiting for transfers between devices: 429 us -> none  [per_device(): lax.psum_scatter(lax.dot_general(onehot, residual, (((0,), (0,)), ((), ()...]
    all_gather x3 -> x0, waiting for transfers between devices: 234 us -> none  [per_device(): gathered = lax.all_gather(updated, 'dp', axis=0, tiled=True)]
    unnamed x8 -> x0, waiting for transfers between devices: 139 us -> none
    pallas_call x0 -> x3, Pallas kernels: none -> 91 us  [the longest x1 88.8 us: per_device(): pl.pallas_call(sections_kernel, out_shape=jax.ShapeDtypeStruct((BLOCKS, R...]
    all_to_all x0 -> x2, blocking collectives: none -> 63.7 us  [the longest x1 40.7 us: per_device(): mine = lax.all_to_all(packed, 'dp', 0, 0, tiled=True)]
    dot_general x3 -> x0, matrix products: 21.5 us -> none  [per_device(): lax.dot_general(onehot, residual, (((0,), (0,)), ((), ())), preferred_ele...]
    scatter-add x3 -> x0, other arithmetic: 17.8 us -> none  [per_device(): jax.ops.segment_sum(weights_wide, code_ids[section_idx], num_segments=CODES)]
    gather x3 -> x0, local copies, waits for them, and re-layouts: 15 us -> none  [per_device(): centroid_rows = jnp.take(gathered, codes_now, axis=0)]
  transfers between devices with their start and end apart: 7 -> 0, of which waited for: 7 -> 0; matrix products, arithmetic and copies ran while one was open for 1% -> 0% of each run, Pallas kernels for 0% -> 0%
where the time goes in v1:
time: 169 us
  Pallas kernels  91 us (54%)
  blocking collectives  74.8 us (44%)
  local copies, waits for them, and re-layouts  2.61 us (2%)
    pallas_call x1, Pallas kernels, per_device(): pl.pallas_call(sections_kernel, out_shape=jax.ShapeDtypeStruct((BLOCKS, R...  88.8 us
    all_to_all x1, blocking collectives, per_device(): mine = lax.all_to_all(packed, 'dp', 0, 0, tiled=True)  40.7 us
    all_to_all x1, blocking collectives, per_device(): back = lax.all_to_all(done, 'dp', 0, 0, tiled=True)  23 us
    psum x1, blocking collectives, per_device(): item_error = lax.psum(error, 'feat').reshape(1024)  11 us

profile of v1, /device:TPU:8, one launch (start us, length us, event | category | flops | bytes accessed | tf_op | source)
XLA Modules:
  0.0 169.0 jit_solution(12721471209232381859)
XLA Ops:
  0.6 0.0 copy-start.2
  0.6 0.7 reshape.15.ids_ref
  1.4 0.0 copy-done.2
  1.4 0.0 copy-start
  1.4 0.9 copy-done
  2.3 0.0 copy-start.1
  2.3 0.9 copy-done.1
  3.3 0.7 pack.1
  4.0 40.7 %all_to_all.10.in_ref = bf16[64,64,128]{2,1,0:T(8,128)(2,1)S(1)} all-to-all(bf16[64,64,128]{2,1,0:T(8,128)(2,1)S(1)} %pack.1), channel_id=1, replica_groups=mesh['dp'=64,'feat'=4] {'dp'}, dimensions={0} | all-to-all | bytes 2097152 | tf_op jit(solution)/shard_map/to_features/all_to_all | solution.py:231
  44.7 88.8 %sections.1 = bf16[64,32,128]{2,1,0:T(8,128)(2,1)S(1)} custom-call(bf16[64,64,128]{2,1,0:T(8,128)(2,1)S(1)} %all_to_all.10.in_ref), custom_call_target="tpu_custom_call" | custom-call | tf_op jit(solution)/shard_map/sections/pallas_call | solution.py:233
  133.5 23.0 %all_to_all.11.in_ref = bf16[64,32,128]{2,1,0:T(8,128)(2,1)S(1)} all-to-all(bf16[64,32,128]{2,1,0:T(8,128)(2,1)S(1)} %sections.1), channel_id=1, replica_groups=mesh['dp'=64,'feat'=4] {'dp'}, dimensions={0} | all-to-all | bytes 1048576 | tf_op jit(solution)/shard_map/to_items/all_to_all | solution.py:249
  156.6 1.4 unpack.1
  158.0 11.0 %psum.7 = f32[1024]{0:T(1024)} all-reduce(f32[1024]{0:T(1024)S(1)} %bitcast.2), channel_id=1, replica_groups=mesh['dp'=64,'feat'=4] {'feat'}, use_global_device_ids=true, to_apply=%region_0.0 | all-reduce | flops 1024 | bytes 8192 | tf_op jit(solution)/shard_map/error/psum | solution.py:265
Async XLA Ops:
  0.6 0.7 copy-start.2
  1.4 1.0 copy-start
  2.3 0.9 copy-start.1

commit v2 on v1

--- a/solution.py
+++ b/solution.py
@@ -12,6 +12,7 @@
 BLOCKS = 64
 FEATS = 128
 prior_weight = 4.0
+GROUP = 4
 
 ROWS_IN = 64
 ROWS_OUT = 32
@@ -22,7 +23,30 @@
     return head, x - head
 
 
-def pack_kernel(emb_ref, ids_ref, w_ref, book_ref, out_ref, emb_rows, book_rows):
+def pack_kernel(
+    emb_hbm, ids_hbm, w_hbm, book_hbm, out_ref, emb_ref, ids_ref, w_ref, book_ref, emb_rows, book_rows,
+    shared_rows, sems
+):
+    pairs = ((ids_hbm, ids_ref), (w_hbm, w_ref), (emb_hbm, emb_ref), (book_hbm, book_ref))
+    copies = [
+        pltpu.make_async_copy(source, target, sems.at[at])
+        for at, (source, target) in enumerate(pairs)
+    ]
+    for copy in copies:
+        copy.start()
+    book_rows[...] = jnp.zeros_like(book_rows)
+    copies[0].wait()
+    ids = ids_ref[...]
+    run = ids >> 7
+    coded = ((ids & 127) + 128).astype(F32)
+    for bit in range(6):
+        coded = coded * jnp.where((run >> bit) & 1 == 1, 2.0 ** (1 << bit), 1.0)
+    for block in range(8):
+        shared_rows[pl.ds(block, SECTIONS, stride=8), :] = coded[:, block * 128 : block * 128 + 128]
+    copies[1].wait()
+    shared_rows[24:32, :] = w_ref[...].astype(F32)
+    shared = shared_rows[...].astype(BF16)
+    copies[2].wait()
     for block in range(8):
         turned = emb_ref[block * 128 : (block + 1) * 128, :].astype(F32).T
         for group in range(16):
@@ -30,7 +54,7 @@
             emb_rows[pl.ds(first * 16 + which * 8 + block, 8, stride=16), :] = turned[
                 group * 8 : (group + 1) * 8
             ]
-    book_rows[...] = jnp.zeros_like(book_rows)
+    copies[3].wait()
     for section in range(SECTIONS):
         parts = two_parts(book_ref[section].T)
         for part in range(2):
@@ -39,20 +63,13 @@
                 book_rows[
                     pl.ds(first * 16 + part * 8 + section * 2 + which, 8, stride=16), :
                 ] = parts[part][group * 8 : (group + 1) * 8]
-    ids = ids_ref[...]
-    run = ids >> 7
-    coded = ((ids & 127) + 128).astype(F32)
-    for bit in range(6):
-        coded = coded * jnp.where((run >> bit) & 1 == 1, 2.0 ** (1 << bit), 1.0)
-    shared = jnp.concatenate([coded, w_ref[...].astype(F32)], axis=0).astype(BF16)
 
     @pl.loop(0, RUNS)
     def _(dest):
-        out_ref[dest, 0:16, :] = emb_rows[pl.ds(pl.multiple_of(dest * 16, 16), 16), :].astype(BF16)
+        at = pl.ds(pl.multiple_of(dest * 16, 16), 16)
+        out_ref[dest, 0:16, :] = emb_rows[at, :].astype(BF16)
         out_ref[dest, 16:48, :] = shared
-        out_ref[dest, 48:64, :] = book_rows[pl.ds(pl.multiple_of(dest * 16, 16), 16), :].astype(
-            BF16
-        )
+        out_ref[dest, 48:64, :] = book_rows[at, :].astype(BF16)
 
 
 def wide_row(ref, row, size):
@@ -60,7 +77,7 @@
 
 
 def sections_kernel(
-    in_ref, out_ref, runs, codes, weights, residual, books_in, books_out, table, total
+    in_ref, out_ref, runs, codes, weights, residual, books_in, books_out, table, total, fresh, stage
 ):
     @pl.loop(0, BLOCKS)
     def _(block):
@@ -87,15 +104,15 @@
     nought = jnp.zeros((16, 128), BF16)
     one = jnp.ones((16, 128), BF16)
 
-    def add_block(section, block):
+    def add_items(section, item_row, source, source_row, count):
         lefts, rights = [], []
-        for row in range(8):
-            at = block * 8 + row
+        for row in range(count):
+            at, source_at = item_row + row, source_row + row
             run = wide_row(runs.at[section], at, 16).astype(BF16)
             code = wide_row(codes.at[section], at, 16).astype(BF16)
             weight = wide_row(weights, at, 16).astype(BF16)
-            first = wide_row(residual.at[0], at, 16).astype(BF16)
-            second = wide_row(residual.at[1], at, 16).astype(BF16)
+            first = wide_row(source.at[0], source_at, 16).astype(BF16)
+            second = wide_row(source.at[1], source_at, 16).astype(BF16)
             masks = [run == iotas[step] for step in range(4)]
             lefts.append(
                 jnp.concatenate(
@@ -128,7 +145,7 @@
             mask = run == float(each)
             for which in range(2):
                 wide = wide_row(table.at[which], each, 8)
-                found = jnp.take_along_axis(wide, code, axis=1)
+                found = jnp.take_along_axis(wide, code, axis=1, mode='promise_in_bounds')
                 rows[which] = jnp.where(mask, found, rows[which])
         result = []
         for which in range(2):
@@ -160,21 +177,32 @@
 
     total[...] = jnp.zeros_like(total)
 
-    @pl.loop(0, BLOCKS)
-    def _(block):
-        add_block(0, block)
+    @pl.loop(0, BLOCKS // 8, unroll=2)
+    def _(group):
+        add_items(0, group * 64, residual, group * 64, 64)
 
     update(0)
     for section in range(1, SECTIONS):
 
-        @pl.loop(0, BLOCKS)
-        def _(block):
-            take_block(section - 1, block)
-            add_block(section, block)
-
+        def take(group, step):
+            left = take_block(section - 1, group * GROUP + step)
+            for which in range(2):
+                fresh[which, 8 * step : 8 * step + 8, :] = left[which].astype(F32)
+
+        for step in range(GROUP):
+            take(0, step)
+
+        @pl.loop(1, BLOCKS // GROUP)
+        def _(group):
+            stage[...] = fresh[...]
+            for step in range(GROUP):
+                take(group, step)
+                add_items(section, ((group - 1) * GROUP + step) * 8, stage, 8 * step, 8)
+
+        add_items(section, (BLOCKS - GROUP) * 8, fresh, 0, 8 * GROUP)
         update(section)
 
-    @pl.loop(0, BLOCKS)
+    @pl.loop(0, BLOCKS, unroll=8)
     def _(block):
         left = take_block(SECTIONS - 1, block)
         out_ref[block, 0:16, :] = jnp.concatenate(left, axis=0)
@@ -183,15 +211,21 @@
         ].astype(BF16)
 
 
-def unpack_kernel(in_ref, book_ref, left_ref, error_ref, left_rows, book_rows):
-    def one(source, error):
+def error_kernel(in_ref, error_ref):
+    def add(source, error):
         rows = in_ref[source, 0:16, :].astype(F32)
+        return error + rows[0:8] * rows[0:8] + rows[8:16] * rows[8:16]
+
+    error_ref[...] = lax.fori_loop(0, RUNS, add, jnp.zeros((8, 128), F32), unroll=8)
+
+
+def unpack_kernel(in_ref, book_ref, left_ref, left_rows, book_rows):
+    @pl.loop(0, RUNS, unroll=8)
+    def _(source):
         at = pl.ds(pl.multiple_of(source * 16, 16), 16)
-        left_rows[at, :] = rows
+        left_rows[at, :] = in_ref[source, 0:16, :].astype(F32)
         book_rows[at, :] = in_ref[source, 16:32, :].astype(F32)
-        return error + rows[0:8] * rows[0:8] + rows[8:16] * rows[8:16]
-
-    error_ref[...] = lax.fori_loop(0, RUNS, one, jnp.zeros((8, 128), F32))
+
     for block in range(8):
         turned = jnp.concatenate(
             [
@@ -215,18 +249,33 @@
         book_ref[section] = turned.T
 
 
+def sum_over_feat(value):
+    one, two, three = [
+        lax.ppermute(value, "feat", [(at, (at + step) % 4) for at in range(4)])
+        for step in range(1, 4)
+    ]
+    return (value + two) + (one + three)
+
+
 def per_device(embeddings, code_ids, codebooks, item_weight):
     params = pltpu.CompilerParams(vmem_limit_bytes=48 * 1024 * 1024)
     with jax.named_scope("pack"):
         packed = pl.pallas_call(
             pack_kernel,
             out_shape=jax.ShapeDtypeStruct((RUNS, ROWS_IN, 128), BF16),
+            in_specs=[pl.BlockSpec(memory_space=pltpu.HBM)] * 4,
             scratch_shapes=[
-                pltpu.VMEM((RUNS * 16, 128), F32),
-                pltpu.VMEM((RUNS * 16, 128), F32),
-            ],
-            compiler_params=params,
-        )(embeddings, code_ids.reshape(24, 128), item_weight.reshape(8, 128), codebooks)
+                pltpu.VMEM((1024, FEATS), BF16),
+                pltpu.VMEM((SECTIONS, 1024), jnp.int32),
+                pltpu.VMEM((8, 128), BF16),
+                pltpu.VMEM((SECTIONS, 128, FEATS), F32),
+                pltpu.VMEM((RUNS * 16, 128), F32),
+                pltpu.VMEM((RUNS * 16, 128), F32),
+                pltpu.VMEM((32, 128), F32),
+                pltpu.SemaphoreType.DMA((4,)),
+            ],
+            compiler_params=pltpu.CompilerParams(vmem_limit_bytes=63 * 1024 * 1024),
+        )(embeddings, code_ids, item_weight.reshape(8, 128), codebooks)
     with jax.named_scope("to_features"):
         mine = lax.all_to_all(packed, "dp", 0, 0, tiled=True)
     with jax.named_scope("sections"):
@@ -242,18 +291,24 @@
                 pltpu.VMEM((RUNS * 16, 128), F32),
                 pltpu.VMEM((2, RUNS, 128), F32),
                 pltpu.VMEM((3 * RUNS, 128), F32),
+                pltpu.VMEM((2, 8 * GROUP, 128), F32),
+                pltpu.VMEM((2, 8 * GROUP, 128), F32),
             ],
             compiler_params=params,
         )(mine)
     with jax.named_scope("to_items"):
         back = lax.all_to_all(done, "dp", 0, 0, tiled=True)
+    with jax.named_scope("error"):
+        error = pl.pallas_call(
+            error_kernel, out_shape=jax.ShapeDtypeStruct((8, 128), F32), compiler_params=params
+        )(back)
+        item_error = sum_over_feat(error).reshape(1024)
     with jax.named_scope("unpack"):
-        updated, left, error = pl.pallas_call(
+        updated, left = pl.pallas_call(
             unpack_kernel,
             out_shape=(
                 jax.ShapeDtypeStruct((SECTIONS, 128, FEATS), F32),
                 jax.ShapeDtypeStruct((1024, FEATS), BF16),
-                jax.ShapeDtypeStruct((8, 128), F32),
             ),
             scratch_shapes=[
                 pltpu.VMEM((RUNS * 16, 128), F32),
@@ -261,8 +316,6 @@
             ],
             compiler_params=params,
         )(back)
-    with jax.named_scope("error"):
-        item_error = lax.psum(error, "feat").reshape(1024)
     return updated, left, item_error
 
 

time: 169 us -> 117 us (0.69)
  Pallas kernels: 91 us -> 44.2 us
  blocking collectives: 74.8 us -> 63.8 us
  starting transfers between devices: 0 us -> 5.13 us
  local copies, waits for them, and re-layouts: 2.61 us -> 0 us
  waiting for transfers between devices: 0 us -> 1.72 us
    pallas_call x1, Pallas kernels: 88.8 us -> 40.2 us  [per_device(): pl.pallas_call(sections_kernel, out_shape=jax.ShapeDtypeStruct((BLOCKS, R...]
    psum x1 -> x0, blocking collectives: 11 us -> none  [per_device(): item_error = lax.psum(error, 'feat').reshape(1024)]
    ppermute x0 -> x3, starting transfers between devices: none -> 5.13 us  [sum_over_feat(): lax.ppermute(value, 'feat', [(at, (at + step) % 4) for at in range(4)])]
    pallas_call x1, Pallas kernels: 0.73 us -> 2.8 us  [per_device(): pl.pallas_call(pack_kernel, out_shape=jax.ShapeDtypeStruct((RUNS, ROWS_IN...]
    unnamed x6 -> x0, local copies, waits for them, and re-layouts: 1.88 us -> none
    ppermute x0 -> x3, waiting for transfers between devices: none -> 1.72 us  [sum_over_feat(): lax.ppermute(value, 'feat', [(at, (at + step) % 4) for at in range(4)])]
  transfers between devices with their start and end apart: 0 -> 3, of which waited for: 0 -> 2; matrix products, arithmetic and copies ran while one was open for 0% -> 0% of each run, Pallas kernels for 0% -> 1%
where the time goes in v2:
time: 117 us; the launch traced here: 116 us
  blocking collectives  63.8 us (55%)
  Pallas kernels  44.2 us (38%)
  starting transfers between devices  5.13 us (4%)
  waiting for transfers between devices  1.72 us (1%)
    all_to_all x1, blocking collectives, per_device(): mine = lax.all_to_all(packed, 'dp', 0, 0, tiled=True)  40.9 us
    pallas_call x1, Pallas kernels, per_device(): pl.pallas_call(sections_kernel, out_shape=jax.ShapeDtypeStruct((BLOCKS, R...  40.2 us
    all_to_all x1, blocking collectives, per_device(): back = lax.all_to_all(done, 'dp', 0, 0, tiled=True)  22.9 us
    ppermute x3, starting transfers between devices, sum_over_feat(): lax.ppermute(value, 'feat', [(at, (at + step) % 4) for at in range(4)])  5.13 us
    pallas_call x1, Pallas kernels, per_device(): pl.pallas_call(pack_kernel, out_shape=jax.ShapeDtypeStruct((RUNS, ROWS_IN...  2.8 us
  transfers between devices with their start and end apart: 3, of which 2 were waited for; matrix products, arithmetic and copies ran while one was open for 0% of the time, Pallas kernels for 1%

profile of v2, /device:TPU:8, one launch (start us, length us, event | category | flops | bytes accessed | tf_op | source)
XLA Modules:
  0.0 116.1 jit_solution(13047865934734824835)
XLA Ops:
  0.6 2.8 %pack.1 = bf16[64,64,128]{2,1,0:T(8,128)(2,1)} custom-call(bf16[1024,128]{1,0:T(8,128)(2,1)} %emb_hbm.1, s32[3,1024]{1,0:T(4,128)} %ids_hbm.1, bf16[8,128]{1,0:T(8,128)(2,1)} %bitcast.3, f32[3,128,128]{2,1,0:T(8,128)} %book_hbm.1), custom_call_target="tpu_custom_call" | custom-call | tf_op jit(solution)/shard_map/pack/pallas_call | solution.py:263
  3.4 40.9 %all_to_all.10.in_ref = bf16[64,64,128]{2,1,0:T(8,128)(2,1)S(1)} all-to-all(bf16[64,64,128]{2,1,0:T(8,128)(2,1)} %pack.1), channel_id=1, replica_groups=mesh['dp'=64,'feat'=4] {'dp'}, dimensions={0} | all-to-all | bytes 2097152 | tf_op jit(solution)/shard_map/to_features/all_to_all | solution.py:280
  44.3 40.2 %sections.1 = bf16[64,32,128]{2,1,0:T(8,128)(2,1)S(1)} custom-call(bf16[64,64,128]{2,1,0:T(8,128)(2,1)S(1)} %all_to_all.10.in_ref), custom_call_target="tpu_custom_call" | custom-call | tf_op jit(solution)/shard_map/sections/pallas_call | solution.py:282
  84.5 22.9 %all_to_all.11.in_ref = bf16[64,32,128]{2,1,0:T(8,128)(2,1)S(1)} all-to-all(bf16[64,32,128]{2,1,0:T(8,128)(2,1)S(1)} %sections.1), channel_id=1, replica_groups=mesh['dp'=64,'feat'=4] {'dp'}, dimensions={0} | all-to-all | bytes 1048576 | tf_op jit(solution)/shard_map/to_items/all_to_all | solution.py:300
  107.4 0.2 error.1
  107.6 2.8 %collective-permute-start.2 = (f32[8,128]{1,0:T(8,128)S(1)}, f32[8,128]{1,0:T(8,128)S(1)}, u32[]{:S(2)}, u32[]{:S(2)}) collective-permute-start(f32[8,128]{1,0:T(8,128)S(1)} %error.1), channel_id=1, source_target_pairs={{0,3},{1,0},{2,1},{3,2},{4,7},{5,4},{6,5},{7,6},{8,11},{9,8},{10,9... | collective-permute-start | bytes 12296 | tf_op jit(solution)/shard_map/error/ppermute | solution.py:254
  110.4 0.0 collective-permute-start.1
  110.4 2.3 %collective-permute-start = (f32[8,128]{1,0:T(8,128)S(1)}, f32[8,128]{1,0:T(8,128)S(1)}, u32[]{:S(2)}, u32[]{:S(2)}) collective-permute-start(f32[8,128]{1,0:T(8,128)S(1)} %error.1), channel_id=1, source_target_pairs={{0,2},{1,3},{2,0},{3,1},{4,6},{5,7},{6,4},{7,5},{8,10},{9,11},{10,... | collective-permute-start | bytes 12296 | tf_op jit(solution)/shard_map/error/ppermute | solution.py:254
  112.7 1.1 unpack.1
  113.8 0.0 collective-permute-done.2
  113.8 1.4 %collective-permute-done.1 = f32[8,128]{1,0:T(8,128)S(1)} collective-permute-done((f32[8,128]{1,0:T(8,128)S(1)}, f32[8,128]{1,0:T(8,128)S(1)}, u32[]{:S(2)}, u32[]{:S(2)}) %collective-permute-start.1) | collective-permute-done | bytes 4128 | tf_op jit(solution)/shard_map/error/ppermute | solution.py:254
  115.2 0.3 collective-permute-done
  115.5 0.6 add_bitcast_fusion
Async XLA Ops:
  107.6 6.2 %collective-permute-start.2 = (f32[8,128]{1,0:T(8,128)S(1)}, f32[8,128]{1,0:T(8,128)S(1)}, u32[]{:S(2)}, u32[]{:S(2)}) collective-permute-start(f32[8,128]{1,0:T(8,128)S(1)} %error.1), channel_id=1, source_target_pairs={{0,3},{1,0},{2,1},{3,2},{4,7},{5,4},{6,5},{7,6},{8,11},{9,8},{10,9... | collective-permute-start | bytes 12296 | tf_op jit(solution)/shard_map/error/ppermute | solution.py:254
  110.4 4.8 %collective-permute-start.1 = (f32[8,128]{1,0:T(8,128)S(1)}, f32[8,128]{1,0:T(8,128)S(1)}, u32[]{:S(2)}, u32[]{:S(2)}) collective-permute-start(f32[8,128]{1,0:T(8,128)S(1)} %error.1), channel_id=1, source_target_pairs={{0,1},{1,2},{2,3},{3,0},{4,5},{5,6},{6,7},{7,4},{8,9},{9,10},{10,1... | collective-permute-start | bytes 12296 | tf_op jit(solution)/shard_map/error/ppermute | solution.py:254
  110.4 5.1 %collective-permute-start = (f32[8,128]{1,0:T(8,128)S(1)}, f32[8,128]{1,0:T(8,128)S(1)}, u32[]{:S(2)}, u32[]{:S(2)}) collective-permute-start(f32[8,128]{1,0:T(8,128)S(1)} %error.1), channel_id=1, source_target_pairs={{0,2},{1,3},{2,0},{3,1},{4,6},{5,7},{6,4},{7,5},{8,10},{9,11},{10,... | collective-permute-start | bytes 12296 | tf_op jit(solution)/shard_map/error/ppermute | solution.py:254

commit v3 on v2

--- a/solution.py
+++ b/solution.py
@@ -12,9 +12,9 @@
 BLOCKS = 64
 FEATS = 128
 prior_weight = 4.0
-GROUP = 4
-
-ROWS_IN = 64
+GROUP = 8
+
+ROWS_IN = 48
 ROWS_OUT = 32
 
 
@@ -64,12 +64,14 @@
                     pl.ds(first * 16 + part * 8 + section * 2 + which, 8, stride=16), :
                 ] = parts[part][group * 8 : (group + 1) * 8]
 
-    @pl.loop(0, RUNS)
-    def _(dest):
-        at = pl.ds(pl.multiple_of(dest * 16, 16), 16)
-        out_ref[dest, 0:16, :] = emb_rows[at, :].astype(BF16)
-        out_ref[dest, 16:48, :] = shared
-        out_ref[dest, 48:64, :] = book_rows[at, :].astype(BF16)
+    @pl.loop(0, RUNS // 2, unroll=4)
+    def _(chip):
+        for core in range(2):
+            dest = chip * 2 + core
+            at = pl.ds(pl.multiple_of(dest * 16, 16), 16)
+            out_ref[dest, 0:16, :] = emb_rows[at, :].astype(BF16)
+            out_ref[dest, 16:32, :] = shared[core * 16 : core * 16 + 16]
+            out_ref[dest, 32:48, :] = book_rows[at, :].astype(BF16)
 
 
 def wide_row(ref, row, size):
@@ -77,17 +79,22 @@
 
 
 def sections_kernel(
-    in_ref, out_ref, runs, codes, weights, residual, books_in, books_out, table, total, fresh, stage
+    in_ref, other_ref, out_ref, runs, codes, weights, residual, books_in, books_out, table, total, fresh, stage, steps
 ):
-    @pl.loop(0, BLOCKS)
+    is_first = lax.axis_index("dp") % 2 == 0
+
+    @pl.loop(0, BLOCKS, unroll=2)
     def _(block):
         at = pl.ds(pl.multiple_of(block * 8, 8), 8)
         values = in_ref[block, 0:16, :].astype(F32)
         residual[0, at, :] = values[0:8]
         residual[1, at, :] = values[8:16]
-        shared = in_ref[block, 16:48, :].astype(F32)
-        weights[at, :] = shared[24:32]
-        coded = shared[0:24]
+        own = in_ref[block, 16:32, :].astype(F32)
+        other = other_ref[block, 16:32, :].astype(F32)
+        first = jnp.where(is_first, own, other)
+        second = jnp.where(is_first, other, own)
+        weights[at, :] = second[8:16]
+        coded = jnp.concatenate([first, second[0:8]], axis=0)
         run = jnp.zeros_like(coded)
         for bit in range(5, -1, -1):
             over = coded >= 128.0 * 2.0 ** (1 << bit)
@@ -96,7 +103,7 @@
         for section in range(SECTIONS):
             runs[section, at, :] = run[section * 8 : section * 8 + 8]
             codes[section, at, :] = coded[section * 8 : section * 8 + 8] - 128.0
-        books_in[pl.ds(pl.multiple_of(block * 16, 16), 16), :] = in_ref[block, 48:64, :].astype(F32)
+        books_in[pl.ds(pl.multiple_of(block * 16, 16), 16), :] = in_ref[block, 32:48, :].astype(F32)
 
     books_out[...] = jnp.zeros_like(books_out)
     down = lax.broadcasted_iota(jnp.int32, (16, 128), 0).astype(F32)
@@ -140,22 +147,25 @@
         at = pl.ds(pl.multiple_of(block * 8, 8), 8)
         run = runs[section, at, :]
         code = codes[section, at, :].astype(jnp.int32)
-        rows = [jnp.zeros((8, 128), F32)] * 2
+        both = jnp.zeros((8, 128), jnp.int32)
         for each in range(RUNS):
-            mask = run == float(each)
-            for which in range(2):
-                wide = wide_row(table.at[which], each, 8)
-                found = jnp.take_along_axis(wide, code, axis=1, mode='promise_in_bounds')
-                rows[which] = jnp.where(mask, found, rows[which])
+            found = jnp.take_along_axis(
+                wide_row(table, each, 8), code, axis=1, mode="promise_in_bounds"
+            )
+            both = jnp.where(run == float(each), found, both)
+        low = (both << 16) >> 16
         result = []
-        for which in range(2):
-            left = (residual[which, at, :] - rows[which]).astype(BF16)
+        for which, whole in enumerate(((both - low) >> 16, low)):
+            row = whole.astype(F32) * steps[which : which + 1, :]
+            left = (residual[which, at, :] - row).astype(BF16)
             residual[which, at, :] = left.astype(F32)
             result.append(left)
         return result
 
     def update(section):
-        count = prior_weight + total[128:192, :]
+        weight = total[128:192, :]
+        count = prior_weight + weight
+        levels = []
         for which in range(2):
             book = jnp.concatenate(
                 [
@@ -166,13 +176,19 @@
                 axis=0,
             )
             new = (prior_weight * book + total[which * 64 : which * 64 + 64, :]) / count
-            table[which] = new
+            used = jnp.where(weight > 0.0, jnp.abs(new), 0.0)
+            largest = jnp.max(jnp.max(used, axis=0, keepdims=True), axis=1, keepdims=True)
+            step = jnp.maximum(largest, 1e-20) * (1.0 / 32767.0)
+            steps[which : which + 1, :] = jnp.broadcast_to(step, (1, 128))
+            level = jnp.clip(new / step, -32767.0, 32767.0)
+            levels.append(jnp.round(level).astype(jnp.int32))
             parts = two_parts(new)
             for part in range(2):
                 for first in range(0, RUNS, 8):
                     books_out[
                         pl.ds(first * 16 + part * 8 + section * 2 + which, 8, stride=16), :
                     ] = parts[part][first : first + 8]
+        table[...] = levels[0] * 65536 + levels[1]
         total[...] = jnp.zeros_like(total)
 
     total[...] = jnp.zeros_like(total)
@@ -278,6 +294,8 @@
         )(embeddings, code_ids, item_weight.reshape(8, 128), codebooks)
     with jax.named_scope("to_features"):
         mine = lax.all_to_all(packed, "dp", 0, 0, tiled=True)
+    with jax.named_scope("to_other_core"):
+        other = lax.ppermute(mine, "dp", [(at, at ^ 1) for at in range(lax.axis_size("dp"))])
     with jax.named_scope("sections"):
         done = pl.pallas_call(
             sections_kernel,
@@ -289,13 +307,14 @@
                 pltpu.VMEM((2, BLOCKS * 8, 128), F32),
                 pltpu.VMEM((RUNS * 16, 128), F32),
                 pltpu.VMEM((RUNS * 16, 128), F32),
-                pltpu.VMEM((2, RUNS, 128), F32),
+                pltpu.VMEM((RUNS, 128), jnp.int32),
                 pltpu.VMEM((3 * RUNS, 128), F32),
                 pltpu.VMEM((2, 8 * GROUP, 128), F32),
                 pltpu.VMEM((2, 8 * GROUP, 128), F32),
+                pltpu.VMEM((8, 128), F32),
             ],
             compiler_params=params,
-        )(mine)
+        )(mine, other)
     with jax.named_scope("to_items"):
         back = lax.all_to_all(done, "dp", 0, 0, tiled=True)
     with jax.named_scope("error"):

time: 117 us -> 104 us (0.89)
  Pallas kernels: 44.2 us -> 34.6 us
  blocking collectives: 63.8 us -> 58.5 us
  waiting for transfers between devices: 1.72 us -> 4 us
    pallas_call x1, Pallas kernels: 40.2 us -> 30.9 us  [per_device(): pl.pallas_call(sections_kernel, out_shape=jax.ShapeDtypeStruct((BLOCKS, R...]
    all_to_all x1, blocking collectives: 40.9 us -> 35.3 us  [per_device(): mine = lax.all_to_all(packed, 'dp', 0, 0, tiled=True)]
    ppermute x0 -> x1, waiting for transfers between devices: none -> 2.28 us  [per_device(): lax.ppermute(mine, 'dp', [(at, at ^ 1) for at in range(lax.axis_size('dp'...]
  transfers between devices with their start and end apart: 3 -> 4, of which waited for: 2 -> 3; matrix products, arithmetic and copies ran while one was open for 0% -> 0% of each run, Pallas kernels for 1% -> 1%
where the time goes in v3:
time: 104 us; the launch traced here: 103 us
  blocking collectives  58.5 us (56%)
  Pallas kernels  34.6 us (33%)
  starting transfers between devices  5.13 us (5%)
  waiting for transfers between devices  4 us (4%)
    all_to_all x1, blocking collectives, per_device(): mine = lax.all_to_all(packed, 'dp', 0, 0, tiled=True)  35.3 us
    pallas_call x1, Pallas kernels, per_device(): pl.pallas_call(sections_kernel, out_shape=jax.ShapeDtypeStruct((BLOCKS, R...  30.9 us
    all_to_all x1, blocking collectives, per_device(): back = lax.all_to_all(done, 'dp', 0, 0, tiled=True)  23.2 us
    ppermute x3, starting transfers between devices, sum_over_feat(): lax.ppermute(value, 'feat', [(at, (at + step) % 4) for at in range(4)])  5.13 us
    pallas_call x1, Pallas kernels, per_device(): pl.pallas_call(pack_kernel, out_shape=jax.ShapeDtypeStruct((RUNS, ROWS_IN...  2.37 us
    ppermute x1, waiting for transfers between devices, per_device(): lax.ppermute(mine, 'dp', [(at, at ^ 1) for at in range(lax.axis_size('dp'...  2.28 us
  transfers between devices with their start and end apart: 4, of which 3 were waited for; matrix products, arithmetic and copies ran while one was open for 0% of the time, Pallas kernels for 1%

profile of v3, /device:TPU:8, one launch (start us, length us, event | category | flops | bytes accessed | tf_op | source)
XLA Modules:
  0.0 103.4 jit_solution(8859849720625942632)
XLA Ops:
  0.6 2.4 %pack.1 = bf16[64,48,128]{2,1,0:T(8,128)(2,1)} custom-call(bf16[1024,128]{1,0:T(8,128)(2,1)} %emb_hbm.1, s32[3,1024]{1,0:T(4,128)} %ids_hbm.1, bf16[8,128]{1,0:T(8,128)(2,1)} %bitcast.3, f32[3,128,128]{2,1,0:T(8,128)} %book_hbm.1), custom_call_target="tpu_custom_call" | custom-call | tf_op jit(solution)/shard_map/pack/pallas_call | solution.py:279
  3.0 35.3 %all_to_all.10.in_ref = bf16[64,48,128]{2,1,0:T(8,128)(2,1)S(1)} all-to-all(bf16[64,48,128]{2,1,0:T(8,128)(2,1)} %pack.1), channel_id=1, replica_groups=mesh['dp'=64,'feat'=4] {'dp'}, dimensions={0} | all-to-all | bytes 1572864 | tf_op jit(solution)/shard_map/to_features/all_to_all | solution.py:296
  38.3 0.0 collective-permute-start
  38.3 2.3 %collective-permute-done.other_ref = bf16[64,48,128]{2,1,0:T(8,128)(2,1)S(1)} collective-permute-done((bf16[64,48,128]{2,1,0:T(8,128)(2,1)S(1)}, bf16[64,48,128]{2,1,0:T(8,128)(2,1)S(1)}, u32[]{:S(2)}, u32[]{:S(2)}) %collective-permute-start) | collective-permute-done | bytes 786464 | tf_op jit(solution)/shard_map/to_other_core/ppermute | solution.py:298
  40.6 30.9 %sections.1 = bf16[64,32,128]{2,1,0:T(8,128)(2,1)S(1)} custom-call(bf16[64,48,128]{2,1,0:T(8,128)(2,1)S(1)} %all_to_all.10.in_ref, bf16[64,48,128]{2,1,0:T(8,128)(2,1)S(1)} %collective-permute-done.other_ref), custom_call_target="tpu_custom_call" | custom-call | tf_op jit(solution)/shard_map/sections/pallas_call | solution.py:300
  71.5 23.2 %all_to_all.11.in_ref = bf16[64,32,128]{2,1,0:T(8,128)(2,1)S(1)} all-to-all(bf16[64,32,128]{2,1,0:T(8,128)(2,1)S(1)} %sections.1), channel_id=1, replica_groups=mesh['dp'=64,'feat'=4] {'dp'}, dimensions={0} | all-to-all | bytes 1048576 | tf_op jit(solution)/shard_map/to_items/all_to_all | solution.py:319
  94.7 0.2 error.1
  94.8 2.8 %collective-permute-start.3 = (f32[8,128]{1,0:T(8,128)S(1)}, f32[8,128]{1,0:T(8,128)S(1)}, u32[]{:S(2)}, u32[]{:S(2)}) collective-permute-start(f32[8,128]{1,0:T(8,128)S(1)} %error.1), channel_id=1, source_target_pairs={{0,3},{1,0},{2,1},{3,2},{4,7},{5,4},{6,5},{7,6},{8,11},{9,8},{10,9... | collective-permute-start | bytes 12296 | tf_op jit(solution)/shard_map/error/ppermute | solution.py:270
  97.7 0.0 collective-permute-start.2
  97.7 2.3 %collective-permute-start.1 = (f32[8,128]{1,0:T(8,128)S(1)}, f32[8,128]{1,0:T(8,128)S(1)}, u32[]{:S(2)}, u32[]{:S(2)}) collective-permute-start(f32[8,128]{1,0:T(8,128)S(1)} %error.1), channel_id=1, source_target_pairs={{0,2},{1,3},{2,0},{3,1},{4,6},{5,7},{6,4},{7,5},{8,10},{9,11},{10,... | collective-permute-start | bytes 12296 | tf_op jit(solution)/shard_map/error/ppermute | solution.py:270
  100.0 1.1 %unpack.1 = (f32[3,128,128]{2,1,0:T(8,128)}, bf16[1024,128]{1,0:T(8,128)(2,1)}) custom-call(bf16[64,32,128]{2,1,0:T(8,128)(2,1)S(1)} %all_to_all.11.in_ref), custom_call_target="tpu_custom_call" | custom-call | tf_op jit(solution)/shard_map/unpack/pallas_call | solution.py:326
  101.1 0.0 collective-permute-done.3
  101.1 1.4 %collective-permute-done.2 = f32[8,128]{1,0:T(8,128)S(1)} collective-permute-done((f32[8,128]{1,0:T(8,128)S(1)}, f32[8,128]{1,0:T(8,128)S(1)}, u32[]{:S(2)}, u32[]{:S(2)}) %collective-permute-start.2) | collective-permute-done | bytes 4128 | tf_op jit(solution)/shard_map/error/ppermute | solution.py:270
  102.5 0.3 collective-permute-done.1
  102.8 0.6 add_bitcast_fusion
Async XLA Ops:
  38.3 2.3 %collective-permute-start = (bf16[64,48,128]{2,1,0:T(8,128)(2,1)S(1)}, bf16[64,48,128]{2,1,0:T(8,128)(2,1)S(1)}, u32[]{:S(2)}, u32[]{:S(2)}) collective-permute-start(bf16[64,48,128]{2,1,0:T(8,128)(2,1)S(1)} %all_to_all.10.in_ref), channel_id=1, source_target_pairs={{0,4},{4,0},{8,12},{12,8},{16,20},{20,16},{24,28},{28,24},{32,36},... | collective-permute-start | bytes 2359304 | tf_op jit(solution)/shard_map/to_other_core/ppermute | solution.py:298
  94.8 6.2 %collective-permute-start.3 = (f32[8,128]{1,0:T(8,128)S(1)}, f32[8,128]{1,0:T(8,128)S(1)}, u32[]{:S(2)}, u32[]{:S(2)}) collective-permute-start(f32[8,128]{1,0:T(8,128)S(1)} %error.1), channel_id=1, source_target_pairs={{0,3},{1,0},{2,1},{3,2},{4,7},{5,4},{6,5},{7,6},{8,11},{9,8},{10,9... | collective-permute-start | bytes 12296 | tf_op jit(solution)/shard_map/error/ppermute | solution.py:270
  97.7 4.8 %collective-permute-start.2 = (f32[8,128]{1,0:T(8,128)S(1)}, f32[8,128]{1,0:T(8,128)S(1)}, u32[]{:S(2)}, u32[]{:S(2)}) collective-permute-start(f32[8,128]{1,0:T(8,128)S(1)} %error.1), channel_id=1, source_target_pairs={{0,1},{1,2},{2,3},{3,0},{4,5},{5,6},{6,7},{7,4},{8,9},{9,10},{10,1... | collective-permute-start | bytes 12296 | tf_op jit(solution)/shard_map/error/ppermute | solution.py:270
  97.7 5.1 %collective-permute-start.1 = (f32[8,128]{1,0:T(8,128)S(1)}, f32[8,128]{1,0:T(8,128)S(1)}, u32[]{:S(2)}, u32[]{:S(2)}) collective-permute-start(f32[8,128]{1,0:T(8,128)S(1)} %error.1), channel_id=1, source_target_pairs={{0,2},{1,3},{2,0},{3,1},{4,6},{5,7},{6,4},{7,5},{8,10},{9,11},{10,... | collective-permute-start | bytes 12296 | tf_op jit(solution)/shard_map/error/ppermute | solution.py:270

commit v4 on v3

--- a/solution.py
+++ b/solution.py
@@ -15,7 +15,7 @@
 GROUP = 8
 
 ROWS_IN = 48
-ROWS_OUT = 32
+ROWS_OUT = 24
 
 
 def two_parts(x):
@@ -182,12 +182,10 @@
             steps[which : which + 1, :] = jnp.broadcast_to(step, (1, 128))
             level = jnp.clip(new / step, -32767.0, 32767.0)
             levels.append(jnp.round(level).astype(jnp.int32))
-            parts = two_parts(new)
-            for part in range(2):
-                for first in range(0, RUNS, 8):
-                    books_out[
-                        pl.ds(first * 16 + part * 8 + section * 2 + which, 8, stride=16), :
-                    ] = parts[part][first : first + 8]
+            for first in range(0, RUNS, 8):
+                books_out[pl.ds(first * 8 + section * 2 + which, 8, stride=8), :] = new[
+                    first : first + 8
+                ]
         table[...] = levels[0] * 65536 + levels[1]
         total[...] = jnp.zeros_like(total)
 
@@ -221,15 +219,14 @@
     @pl.loop(0, BLOCKS, unroll=8)
     def _(block):
         left = take_block(SECTIONS - 1, block)
-        out_ref[block, 0:16, :] = jnp.concatenate(left, axis=0)
-        out_ref[block, 16:32, :] = books_out[
-            pl.ds(pl.multiple_of(block * 16, 16), 16), :
-        ].astype(BF16)
+        books = books_out[pl.ds(pl.multiple_of(block * 8, 8), 8), :]
+        rows = [left[0].astype(F32), left[1].astype(F32), books]
+        out_ref[block] = jnp.concatenate(rows, axis=0).astype(BF16)
 
 
 def error_kernel(in_ref, error_ref):
     def add(source, error):
-        rows = in_ref[source, 0:16, :].astype(F32)
+        rows = in_ref[source].astype(F32)
         return error + rows[0:8] * rows[0:8] + rows[8:16] * rows[8:16]
 
     error_ref[...] = lax.fori_loop(0, RUNS, add, jnp.zeros((8, 128), F32), unroll=8)
@@ -238,9 +235,9 @@
 def unpack_kernel(in_ref, book_ref, left_ref, left_rows, book_rows):
     @pl.loop(0, RUNS, unroll=8)
     def _(source):
-        at = pl.ds(pl.multiple_of(source * 16, 16), 16)
-        left_rows[at, :] = in_ref[source, 0:16, :].astype(F32)
-        book_rows[at, :] = in_ref[source, 16:32, :].astype(F32)
+        rows = in_ref[source].astype(F32)
+        left_rows[pl.ds(pl.multiple_of(source * 16, 16), 16), :] = rows[0:16]
+        book_rows[pl.ds(pl.multiple_of(source * 8, 8), 8), :] = rows[16:24]
 
     for block in range(8):
         turned = jnp.concatenate(
@@ -255,8 +252,7 @@
     for section in range(SECTIONS):
         turned = jnp.concatenate(
             [
-                book_rows[pl.ds(first * 16 + section * 2 + which, 8, stride=16), :]
-                + book_rows[pl.ds(first * 16 + 8 + section * 2 + which, 8, stride=16), :]
+                book_rows[pl.ds(first * 8 + section * 2 + which, 8, stride=8), :]
                 for which in range(2)
                 for first in range(0, RUNS, 8)
             ],
@@ -306,7 +302,7 @@
                 pltpu.VMEM((BLOCKS * 8, 128), F32),
                 pltpu.VMEM((2, BLOCKS * 8, 128), F32),
                 pltpu.VMEM((RUNS * 16, 128), F32),
-                pltpu.VMEM((RUNS * 16, 128), F32),
+                pltpu.VMEM((RUNS * 8, 128), F32),
                 pltpu.VMEM((RUNS, 128), jnp.int32),
                 pltpu.VMEM((3 * RUNS, 128), F32),
                 pltpu.VMEM((2, 8 * GROUP, 128), F32),
@@ -331,7 +327,7 @@
             ),
             scratch_shapes=[
                 pltpu.VMEM((RUNS * 16, 128), F32),
-                pltpu.VMEM((RUNS * 16, 128), F32),
+                pltpu.VMEM((RUNS * 8, 128), F32),
             ],
             compiler_params=params,
         )(back)

time: 104 us -> 101 us (0.971)
  blocking collectives: 58.5 us -> 55.7 us
    all_to_all x1, blocking collectives: 23.2 us -> 20.4 us  [per_device(): back = lax.all_to_all(done, 'dp', 0, 0, tiled=True)]
where the time goes in v4:
time: 101 us; the launch traced here: 100 us
  blocking collectives  55.7 us (55%)
  Pallas kernels  34.4 us (34%)
  starting transfers between devices  5.12 us (5%)
  waiting for transfers between devices  4.05 us (4%)
    all_to_all x1, blocking collectives, per_device(): mine = lax.all_to_all(packed, 'dp', 0, 0, tiled=True)  35.3 us
    pallas_call x1, Pallas kernels, per_device(): pl.pallas_call(sections_kernel, out_shape=jax.ShapeDtypeStruct((BLOCKS, R...  30.8 us
    all_to_all x1, blocking collectives, per_device(): back = lax.all_to_all(done, 'dp', 0, 0, tiled=True)  20.4 us
    ppermute x3, starting transfers between devices, sum_over_feat(): lax.ppermute(value, 'feat', [(at, (at + step) % 4) for at in range(4)])  5.12 us
    pallas_call x1, Pallas kernels, per_device(): pl.pallas_call(pack_kernel, out_shape=jax.ShapeDtypeStruct((RUNS, ROWS_IN...  2.37 us
    ppermute x1, waiting for transfers between devices, per_device(): lax.ppermute(mine, 'dp', [(at, at ^ 1) for at in range(lax.axis_size('dp'...  2.28 us
  transfers between devices with their start and end apart: 4, of which 3 were waited for; matrix products, arithmetic and copies ran while one was open for 0% of the time, Pallas kernels for 1%

profile of v4, /device:TPU:8, one launch (start us, length us, event | category | flops | bytes accessed | tf_op | source)
XLA Modules:
  0.0 100.5 jit_solution(1393506386661406699)
XLA Ops:
  0.6 2.4 %pack.1 = bf16[64,48,128]{2,1,0:T(8,128)(2,1)} custom-call(bf16[1024,128]{1,0:T(8,128)(2,1)} %emb_hbm.1, s32[3,1024]{1,0:T(4,128)} %ids_hbm.1, bf16[8,128]{1,0:T(8,128)(2,1)} %bitcast.3, f32[3,128,128]{2,1,0:T(8,128)} %book_hbm.1), custom_call_target="tpu_custom_call" | custom-call | tf_op jit(solution)/shard_map/pack/pallas_call | solution.py:275
  3.0 35.3 %all_to_all.10.in_ref = bf16[64,48,128]{2,1,0:T(8,128)(2,1)S(1)} all-to-all(bf16[64,48,128]{2,1,0:T(8,128)(2,1)} %pack.1), channel_id=1, replica_groups=mesh['dp'=64,'feat'=4] {'dp'}, dimensions={0} | all-to-all | bytes 1572864 | tf_op jit(solution)/shard_map/to_features/all_to_all | solution.py:292
  38.3 0.0 collective-permute-start
  38.3 2.3 %collective-permute-done.other_ref = bf16[64,48,128]{2,1,0:T(8,128)(2,1)S(1)} collective-permute-done((bf16[64,48,128]{2,1,0:T(8,128)(2,1)S(1)}, bf16[64,48,128]{2,1,0:T(8,128)(2,1)S(1)}, u32[]{:S(2)}, u32[]{:S(2)}) %collective-permute-start) | collective-permute-done | bytes 786464 | tf_op jit(solution)/shard_map/to_other_core/ppermute | solution.py:294
  40.6 30.8 %sections.1 = bf16[64,24,128]{2,1,0:T(8,128)(2,1)S(1)} custom-call(bf16[64,48,128]{2,1,0:T(8,128)(2,1)S(1)} %all_to_all.10.in_ref, bf16[64,48,128]{2,1,0:T(8,128)(2,1)S(1)} %collective-permute-done.other_ref), custom_call_target="tpu_custom_call" | custom-call | tf_op jit(solution)/shard_map/sections/pallas_call | solution.py:296
  71.4 20.4 %all_to_all.11.in_ref = bf16[64,24,128]{2,1,0:T(8,128)(2,1)S(1)} all-to-all(bf16[64,24,128]{2,1,0:T(8,128)(2,1)S(1)} %sections.1), channel_id=1, replica_groups=mesh['dp'=64,'feat'=4] {'dp'}, dimensions={0} | all-to-all | bytes 786432 | tf_op jit(solution)/shard_map/to_items/all_to_all | solution.py:315
  91.8 0.2 error.1
  91.9 2.8 %collective-permute-start.3 = (f32[8,128]{1,0:T(8,128)S(1)}, f32[8,128]{1,0:T(8,128)S(1)}, u32[]{:S(2)}, u32[]{:S(2)}) collective-permute-start(f32[8,128]{1,0:T(8,128)S(1)} %error.1), channel_id=1, source_target_pairs={{0,3},{1,0},{2,1},{3,2},{4,7},{5,4},{6,5},{7,6},{8,11},{9,8},{10,9... | collective-permute-start | bytes 12296 | tf_op jit(solution)/shard_map/error/ppermute | solution.py:266
  94.8 0.0 collective-permute-start.2
  94.8 2.3 %collective-permute-start.1 = (f32[8,128]{1,0:T(8,128)S(1)}, f32[8,128]{1,0:T(8,128)S(1)}, u32[]{:S(2)}, u32[]{:S(2)}) collective-permute-start(f32[8,128]{1,0:T(8,128)S(1)} %error.1), channel_id=1, source_target_pairs={{0,2},{1,3},{2,0},{3,1},{4,6},{5,7},{6,4},{7,5},{8,10},{9,11},{10,... | collective-permute-start | bytes 12296 | tf_op jit(solution)/shard_map/error/ppermute | solution.py:266
  97.1 1.1 %unpack.1 = (f32[3,128,128]{2,1,0:T(8,128)}, bf16[1024,128]{1,0:T(8,128)(2,1)}) custom-call(bf16[64,24,128]{2,1,0:T(8,128)(2,1)S(1)} %all_to_all.11.in_ref), custom_call_target="tpu_custom_call" | custom-call | tf_op jit(solution)/shard_map/unpack/pallas_call | solution.py:322
  98.1 0.0 collective-permute-done.3
  98.1 1.5 %collective-permute-done.2 = f32[8,128]{1,0:T(8,128)S(1)} collective-permute-done((f32[8,128]{1,0:T(8,128)S(1)}, f32[8,128]{1,0:T(8,128)S(1)}, u32[]{:S(2)}, u32[]{:S(2)}) %collective-permute-start.2) | collective-permute-done | bytes 4128 | tf_op jit(solution)/shard_map/error/ppermute | solution.py:266
  99.6 0.3 collective-permute-done.1
  99.9 0.6 add_bitcast_fusion
Async XLA Ops:
  38.3 2.3 %collective-permute-start = (bf16[64,48,128]{2,1,0:T(8,128)(2,1)S(1)}, bf16[64,48,128]{2,1,0:T(8,128)(2,1)S(1)}, u32[]{:S(2)}, u32[]{:S(2)}) collective-permute-start(bf16[64,48,128]{2,1,0:T(8,128)(2,1)S(1)} %all_to_all.10.in_ref), channel_id=1, source_target_pairs={{0,4},{4,0},{8,12},{12,8},{16,20},{20,16},{24,28},{28,24},{32,36},... | collective-permute-start | bytes 2359304 | tf_op jit(solution)/shard_map/to_other_core/ppermute | solution.py:294
  91.9 6.2 %collective-permute-start.3 = (f32[8,128]{1,0:T(8,128)S(1)}, f32[8,128]{1,0:T(8,128)S(1)}, u32[]{:S(2)}, u32[]{:S(2)}) collective-permute-start(f32[8,128]{1,0:T(8,128)S(1)} %error.1), channel_id=1, source_target_pairs={{0,3},{1,0},{2,1},{3,2},{4,7},{5,4},{6,5},{7,6},{8,11},{9,8},{10,9... | collective-permute-start | bytes 12296 | tf_op jit(solution)/shard_map/error/ppermute | solution.py:266
  94.8 4.8 %collective-permute-start.2 = (f32[8,128]{1,0:T(8,128)S(1)}, f32[8,128]{1,0:T(8,128)S(1)}, u32[]{:S(2)}, u32[]{:S(2)}) collective-permute-start(f32[8,128]{1,0:T(8,128)S(1)} %error.1), channel_id=1, source_target_pairs={{0,1},{1,2},{2,3},{3,0},{4,5},{5,6},{6,7},{7,4},{8,9},{9,10},{10,1... | collective-permute-start | bytes 12296 | tf_op jit(solution)/shard_map/error/ppermute | solution.py:266
  94.8 5.1 %collective-permute-start.1 = (f32[8,128]{1,0:T(8,128)S(1)}, f32[8,128]{1,0:T(8,128)S(1)}, u32[]{:S(2)}, u32[]{:S(2)}) collective-permute-start(f32[8,128]{1,0:T(8,128)S(1)} %error.1), channel_id=1, source_target_pairs={{0,2},{1,3},{2,0},{3,1},{4,6},{5,7},{6,4},{7,5},{8,10},{9,11},{10,... | collective-permute-start | bytes 12296 | tf_op jit(solution)/shard_map/error/ppermute | solution.py:266

commit v5 on v4

--- a/solution.py
+++ b/solution.py
@@ -3,6 +3,7 @@
 from jax import lax
 from jax.experimental import pallas as pl
 from jax.experimental.pallas import tpu as pltpu
+from jax.sharding import Mesh
 from jax.sharding import PartitionSpec as P
 
 F32 = jnp.float32
@@ -14,7 +15,8 @@
 prior_weight = 4.0
 GROUP = 8
 
-ROWS_IN = 48
+CHIPS = 32
+ROWS_IN = 88
 ROWS_OUT = 24
 
 
@@ -45,7 +47,6 @@
         shared_rows[pl.ds(block, SECTIONS, stride=8), :] = coded[:, block * 128 : block * 128 + 128]
     copies[1].wait()
     shared_rows[24:32, :] = w_ref[...].astype(F32)
-    shared = shared_rows[...].astype(BF16)
     copies[2].wait()
     for block in range(8):
         turned = emb_ref[block * 128 : (block + 1) * 128, :].astype(F32).T
@@ -61,51 +62,44 @@
             for group in range(16):
                 which, first = group // 8, (group % 8) * 8
                 book_rows[
-                    pl.ds(first * 16 + part * 8 + section * 2 + which, 8, stride=16), :
+                    pl.ds(first * 16 + part * 6 + section * 2 + which, 8, stride=16), :
                 ] = parts[part][group * 8 : (group + 1) * 8]
 
-    @pl.loop(0, RUNS // 2, unroll=4)
+    shared = shared_rows[...]
+
+    @pl.loop(0, CHIPS, unroll=4)
     def _(chip):
-        for core in range(2):
-            dest = chip * 2 + core
-            at = pl.ds(pl.multiple_of(dest * 16, 16), 16)
-            out_ref[dest, 0:16, :] = emb_rows[at, :].astype(BF16)
-            out_ref[dest, 16:32, :] = shared[core * 16 : core * 16 + 16]
-            out_ref[dest, 32:48, :] = book_rows[at, :].astype(BF16)
+        at = pl.ds(pl.multiple_of(chip * 32, 32), 32)
+        books = book_rows[at, :]
+        rows = [emb_rows[at, :], shared, books[0:8], books[16:24], books[8:12], books[24:28]]
+        out_ref[chip] = jnp.concatenate(rows, axis=0).astype(BF16)
+
+
+def open_chip(rows, is_first):
+    rows = rows.astype(F32)
+    values = jnp.where(is_first, rows[0:16], rows[16:32])
+    last = jnp.concatenate([rows[84:88], rows[80:84]], axis=0)
+    books = [
+        jnp.where(is_first, rows[64:72], rows[72:80]),
+        jnp.where(is_first, rows[80:88], last),
+    ]
+    return values, rows[32:56], rows[56:64], jnp.concatenate(books, axis=0)
+
+
+def run_and_code(coded):
+    run = jnp.zeros_like(coded)
+    for bit in range(5, -1, -1):
+        over = coded >= 128.0 * 2.0 ** (1 << bit)
+        coded = jnp.where(over, coded * 2.0 ** -(1 << bit), coded)
+        run = run + jnp.where(over, float(1 << bit), 0.0)
+    return run, coded - 128.0
 
 
 def wide_row(ref, row, size):
     return jnp.broadcast_to(ref[pl.ds(row, 1), :], (size, 128))
 
 
-def sections_kernel(
-    in_ref, other_ref, out_ref, runs, codes, weights, residual, books_in, books_out, table, total, fresh, stage, steps
-):
-    is_first = lax.axis_index("dp") % 2 == 0
-
-    @pl.loop(0, BLOCKS, unroll=2)
-    def _(block):
-        at = pl.ds(pl.multiple_of(block * 8, 8), 8)
-        values = in_ref[block, 0:16, :].astype(F32)
-        residual[0, at, :] = values[0:8]
-        residual[1, at, :] = values[8:16]
-        own = in_ref[block, 16:32, :].astype(F32)
-        other = other_ref[block, 16:32, :].astype(F32)
-        first = jnp.where(is_first, own, other)
-        second = jnp.where(is_first, other, own)
-        weights[at, :] = second[8:16]
-        coded = jnp.concatenate([first, second[0:8]], axis=0)
-        run = jnp.zeros_like(coded)
-        for bit in range(5, -1, -1):
-            over = coded >= 128.0 * 2.0 ** (1 << bit)
-            coded = jnp.where(over, coded * 2.0 ** -(1 << bit), coded)
-            run = run + jnp.where(over, float(1 << bit), 0.0)
-        for section in range(SECTIONS):
-            runs[section, at, :] = run[section * 8 : section * 8 + 8]
-            codes[section, at, :] = coded[section * 8 : section * 8 + 8] - 128.0
-        books_in[pl.ds(pl.multiple_of(block * 16, 16), 16), :] = in_ref[block, 32:48, :].astype(F32)
-
-    books_out[...] = jnp.zeros_like(books_out)
+def adder(runs, codes, weights, total):
     down = lax.broadcasted_iota(jnp.int32, (16, 128), 0).astype(F32)
     iotas = [(down + 16.0 * step).astype(BF16) for step in range(8)]
     nought = jnp.zeros((16, 128), BF16)
@@ -143,6 +137,55 @@
             preferred_element_type=F32,
         )
 
+    return add_items
+
+
+def first_kernel(in_ref, total, runs, codes, weights, residual):
+    is_first = lax.axis_index("core") == 0
+
+    @pl.loop(0, CHIPS, unroll=2)
+    def _(chip):
+        at = pl.ds(pl.multiple_of(chip * 8, 8), 8)
+        values, coded, weight, _ = open_chip(in_ref[chip], is_first)
+        residual[0, at, :] = values[0:8]
+        residual[1, at, :] = values[8:16]
+        weights[at, :] = weight
+        runs[0, at, :], codes[0, at, :] = run_and_code(coded[0:8])
+
+    add_items = adder(runs, codes, weights, total)
+    total[...] = jnp.zeros_like(total)
+
+    @pl.loop(0, CHIPS // 8, unroll=2)
+    def _(group):
+        add_items(0, group * 64, residual, group * 64, 64)
+
+
+def sections_kernel(
+    in_ref, other_ref, first_ref, out_ref, runs, codes, weights, residual, books_in, books_out, table, total,
+    fresh, stage, steps
+):
+    core = lax.axis_index("core")
+    is_first = core == 0
+
+    for half, ref in enumerate((in_ref, other_ref)):
+
+        @pl.loop(0, CHIPS, unroll=2)
+        def _(chip):
+            at = pl.ds(pl.multiple_of((half * CHIPS + chip) * 8, 8), 8)
+            values, coded, weight, books = open_chip(ref[chip], is_first)
+            residual[0, at, :] = values[0:8]
+            residual[1, at, :] = values[8:16]
+            weights[at, :] = weight
+            run, code = run_and_code(coded)
+            for section in range(SECTIONS):
+                runs[section, at, :] = run[section * 8 : section * 8 + 8]
+                codes[section, at, :] = code[section * 8 : section * 8 + 8]
+            source = chip * 2 + (core if half == 0 else 1 - core)
+            books_in[pl.ds(pl.multiple_of(source * 16, 16), 16), :] = books
+
+    books_out[...] = jnp.zeros_like(books_out)
+    add_items = adder(runs, codes, weights, total)
+
     def take_block(section, block):
         at = pl.ds(pl.multiple_of(block * 8, 8), 8)
         run = runs[section, at, :]
@@ -170,7 +213,7 @@
             book = jnp.concatenate(
                 [
                     books_in[pl.ds(first * 16 + section * 2 + which, 8, stride=16), :]
-                    + books_in[pl.ds(first * 16 + 8 + section * 2 + which, 8, stride=16), :]
+                    + books_in[pl.ds(first * 16 + 6 + section * 2 + which, 8, stride=16), :]
                     for first in range(0, RUNS, 8)
                 ],
                 axis=0,
@@ -189,9 +232,9 @@
         table[...] = levels[0] * 65536 + levels[1]
         total[...] = jnp.zeros_like(total)
 
-    total[...] = jnp.zeros_like(total)
-
-    @pl.loop(0, BLOCKS // 8, unroll=2)
+    total[...] = first_ref[...]
+
+    @pl.loop(CHIPS // 8, BLOCKS // 8, unroll=2)
     def _(group):
         add_items(0, group * 64, residual, group * 64, 64)
 
@@ -216,12 +259,15 @@
         add_items(section, (BLOCKS - GROUP) * 8, fresh, 0, 8 * GROUP)
         update(section)
 
-    @pl.loop(0, BLOCKS, unroll=8)
-    def _(block):
-        left = take_block(SECTIONS - 1, block)
-        books = books_out[pl.ds(pl.multiple_of(block * 8, 8), 8), :]
-        rows = [left[0].astype(F32), left[1].astype(F32), books]
-        out_ref[block] = jnp.concatenate(rows, axis=0).astype(BF16)
+    for half in range(2):
+
+        @pl.loop(0, CHIPS, unroll=8)
+        def _(chip):
+            left = take_block(SECTIONS - 1, half * CHIPS + chip)
+            source = chip * 2 + (core if half == 0 else 1 - core)
+            books = books_out[pl.ds(pl.multiple_of(source * 8, 8), 8), :]
+            rows = [left[0].astype(F32), left[1].astype(F32), books]
+            out_ref[source] = jnp.concatenate(rows, axis=0).astype(BF16)
 
 
 def error_kernel(in_ref, error_ref):
@@ -274,7 +320,7 @@
     with jax.named_scope("pack"):
         packed = pl.pallas_call(
             pack_kernel,
-            out_shape=jax.ShapeDtypeStruct((RUNS, ROWS_IN, 128), BF16),
+            out_shape=jax.ShapeDtypeStruct((CHIPS, ROWS_IN, 128), BF16),
             in_specs=[pl.BlockSpec(memory_space=pltpu.HBM)] * 4,
             scratch_shapes=[
                 pltpu.VMEM((1024, FEATS), BF16),
@@ -289,9 +335,24 @@
             compiler_params=pltpu.CompilerParams(vmem_limit_bytes=63 * 1024 * 1024),
         )(embeddings, code_ids, item_weight.reshape(8, 128), codebooks)
     with jax.named_scope("to_features"):
-        mine = lax.all_to_all(packed, "dp", 0, 0, tiled=True)
+        mine = lax.all_to_all(packed, "chip", 0, 0, tiled=True)
     with jax.named_scope("to_other_core"):
-        other = lax.ppermute(mine, "dp", [(at, at ^ 1) for at in range(lax.axis_size("dp"))])
+        other = lax.ppermute(mine, "core", [(0, 1), (1, 0)])
+    with jax.named_scope("first_sums"):
+        first = pl.pallas_call(
+            first_kernel,
+            out_shape=jax.ShapeDtypeStruct((3 * RUNS, 128), F32),
+            scratch_shapes=[
+                pltpu.VMEM((1, CHIPS * 8, 128), F32),
+                pltpu.VMEM((1, CHIPS * 8, 128), F32),
+                pltpu.VMEM((CHIPS * 8, 128), F32),
+                pltpu.VMEM((2, CHIPS * 8, 128), F32),
+            ],
+            compiler_params=params,
+            cost_estimate=pl.CostEstimate(
+                flops=2 * 3 * RUNS * 128 * CHIPS * 1024, bytes_accessed=2**20, transcendentals=0
+            ),
+        )(mine)
     with jax.named_scope("sections"):
         done = pl.pallas_call(
             sections_kernel,
@@ -310,9 +371,9 @@
                 pltpu.VMEM((8, 128), F32),
             ],
             compiler_params=params,
-        )(mine, other)
+        )(mine, other, first)
     with jax.named_scope("to_items"):
-        back = lax.all_to_all(done, "dp", 0, 0, tiled=True)
+        back = lax.all_to_all(done, ("chip", "core"), 0, 0, tiled=True)
     with jax.named_scope("error"):
         error = pl.pallas_call(
             error_kernel, out_shape=jax.ShapeDtypeStruct((8, 128), F32), compiler_params=params
@@ -335,8 +396,11 @@
 
 
 def solution(mesh):
-    in_specs = (P("dp", "feat"), P(None, "dp"), P(None, "dp", "feat"), P("dp"))
-    out_specs = (P(None, "dp", "feat"), P("dp", "feat"), P("dp"))
+    dp, feat = mesh.devices.shape
+    split = Mesh(mesh.devices.reshape(dp // 2, 2, feat), ("chip", "core", "feat"))
+    dp_axes = ("chip", "core")
+    in_specs = (P(dp_axes, "feat"), P(None, dp_axes), P(None, dp_axes, "feat"), P(dp_axes))
+    out_specs = (P(None, dp_axes, "feat"), P(dp_axes, "feat"), P(dp_axes))
     return jax.shard_map(
-        per_device, mesh=mesh, in_specs=in_specs, out_specs=out_specs, check_vma=False
+        per_device, mesh=split, in_specs=in_specs, out_specs=out_specs, check_vma=False
     )

time: 101 us -> 97.1 us (0.961)
  blocking collectives: 55.7 us -> 53.4 us
  waiting for transfers between devices: 4.05 us -> 1.76 us
    pallas_call x1 -> x2, Pallas kernels: 2.37 us -> 6.19 us  [the longest x1 3.83 us: per_device(): pl.pallas_call(first_kernel, out_shape=jax.ShapeDtypeStruct((3 * RUNS, 12...]
    pallas_call x1, Pallas kernels: 30.8 us -> 27.2 us  [per_device(): pl.pallas_call(sections_kernel, out_shape=jax.ShapeDtypeStruct((BLOCKS, R...]
    ppermute x1, waiting for transfers between devices: 2.28 us -> 0.01 us  [per_device(): other = lax.ppermute(mine, 'core', [(0, 1), (1, 0)])]
    all_to_all x2, blocking collectives: 55.7 us -> 53.4 us  [the longest x1 32.8 us: per_device(): mine = lax.all_to_all(packed, 'chip', 0, 0, tiled=True)]
  transfers between devices with their start and end apart: 4 -> 4, of which waited for: 3 -> 2; matrix products, arithmetic and copies ran while one was open for 0% -> 0% of each run, Pallas kernels for 1% -> 5%
where the time goes in v5:
time: 97.1 us; the launch traced here: 96.2 us
  blocking collectives  53.4 us (55%)
  Pallas kernels  34.7 us (36%)
  starting transfers between devices  5.13 us (5%)
  waiting for transfers between devices  1.76 us (2%)
    all_to_all x1, blocking collectives, per_device(): mine = lax.all_to_all(packed, 'chip', 0, 0, tiled=True)  32.8 us
    pallas_call x1, Pallas kernels, per_device(): pl.pallas_call(sections_kernel, out_shape=jax.ShapeDtypeStruct((BLOCKS, R...  27.2 us
    all_to_all x1, blocking collectives, per_device(): back = lax.all_to_all(done, ('chip', 'core'), 0, 0, tiled=True)  20.6 us
    ppermute x3, starting transfers between devices, sum_over_feat(): lax.ppermute(value, 'feat', [(at, (at + step) % 4) for at in range(4)])  5.13 us
    pallas_call x1, Pallas kernels, per_device(): pl.pallas_call(first_kernel, out_shape=jax.ShapeDtypeStruct((3 * RUNS, 12...  3.83 us
    pallas_call x1, Pallas kernels, per_device(): pl.pallas_call(pack_kernel, out_shape=jax.ShapeDtypeStruct((CHIPS, ROWS_I...  2.36 us
  transfers between devices with their start and end apart: 4, of which 2 were waited for; matrix products, arithmetic and copies ran while one was open for 0% of the time, Pallas kernels for 5%

profile of v5, /device:TPU:8, one launch (start us, length us, event | category | flops | bytes accessed | tf_op | source)
XLA Modules:
  0.0 96.2 jit_solution(1566442648932692868)
XLA Ops:
  0.6 2.4 %pack.1 = bf16[32,88,128]{2,1,0:T(8,128)(2,1)} custom-call(bf16[1024,128]{1,0:T(8,128)(2,1)} %emb_hbm.1, s32[3,1024]{1,0:T(4,128)} %ids_hbm.1, bf16[8,128]{1,0:T(8,128)(2,1)} %bitcast.3, f32[3,128,128]{2,1,0:T(8,128)} %book_hbm.1), custom_call_target="tpu_custom_call" | custom-call | tf_op jit(solution)/shard_map/pack/pallas_call | solution.py:321
  3.0 32.8 %all_to_all.10.in_ref = bf16[32,88,128]{2,1,0:T(8,128)(2,1)S(1)} all-to-all(bf16[32,88,128]{2,1,0:T(8,128)(2,1)} %pack.1), channel_id=1, replica_groups=mesh['chip'=32,'core'=2,'feat'=4] {'chip'}, dimensions={0} | all-to-all | bytes 1441792 | tf_op jit(solution)/shard_map/to_features/all_to_all | solution.py:338
  35.8 0.0 collective-permute-start
  35.8 3.8 %first_sums.1.first_ref = f32[192,128]{1,0:T(8,128)S(1)} custom-call(bf16[32,88,128]{2,1,0:T(8,128)(2,1)S(1)} %all_to_all.10.in_ref), custom_call_target="tpu_custom_call" | custom-call | flops 1610612736 | bytes 1048576 | tf_op jit(solution)/shard_map/first_sums/pallas_call | solution.py:342
  39.6 0.0 collective-permute-done.other_ref
  39.6 27.2 %sections.1 = bf16[64,24,128]{2,1,0:T(8,128)(2,1)S(1)} custom-call(bf16[32,88,128]{2,1,0:T(8,128)(2,1)S(1)} %all_to_all.10.in_ref, bf16[32,88,128]{2,1,0:T(8,128)(2,1)S(1)} %collective-permute-done.other_ref, f32[192,128]{1,0:T(8,128)S(1)} %first_sums.1.first_ref), custom_call_target="tpu_custom_call" | custom-call | tf_op jit(solution)/shard_map/sections/pallas_call | solution.py:357
  66.9 20.6 %all_to_all.11.in_ref = bf16[64,24,128]{2,1,0:T(8,128)(2,1)S(1)} all-to-all(bf16[64,24,128]{2,1,0:T(8,128)(2,1)S(1)} %sections.1), channel_id=1, replica_groups=mesh['chip'=32,'core'=2,'feat'=4] {'chip','core'}, dimensions={0} | all-to-all | bytes 786432 | tf_op jit(solution)/shard_map/to_items/all_to_all | solution.py:376
  87.5 0.2 error.1
  87.6 2.8 %collective-permute-start.3 = (f32[8,128]{1,0:T(8,128)S(1)}, f32[8,128]{1,0:T(8,128)S(1)}, u32[]{:S(2)}, u32[]{:S(2)}) collective-permute-start(f32[8,128]{1,0:T(8,128)S(1)} %error.1), channel_id=1, source_target_pairs={{0,3},{1,0},{2,1},{3,2},{4,7},{5,4},{6,5},{7,6},{8,11},{9,8},{10,9... | collective-permute-start | bytes 12296 | tf_op jit(solution)/shard_map/error/ppermute | solution.py:312
  90.5 0.0 collective-permute-start.2
  90.5 2.3 %collective-permute-start.1 = (f32[8,128]{1,0:T(8,128)S(1)}, f32[8,128]{1,0:T(8,128)S(1)}, u32[]{:S(2)}, u32[]{:S(2)}) collective-permute-start(f32[8,128]{1,0:T(8,128)S(1)} %error.1), channel_id=1, source_target_pairs={{0,2},{1,3},{2,0},{3,1},{4,6},{5,7},{6,4},{7,5},{8,10},{9,11},{10,... | collective-permute-start | bytes 12296 | tf_op jit(solution)/shard_map/error/ppermute | solution.py:312
  92.8 1.1 %unpack.1 = (f32[3,128,128]{2,1,0:T(8,128)}, bf16[1024,128]{1,0:T(8,128)(2,1)}) custom-call(bf16[64,24,128]{2,1,0:T(8,128)(2,1)S(1)} %all_to_all.11.in_ref), custom_call_target="tpu_custom_call" | custom-call | tf_op jit(solution)/shard_map/unpack/pallas_call | solution.py:383
  93.8 0.0 collective-permute-done.3
  93.8 1.5 %collective-permute-done.2 = f32[8,128]{1,0:T(8,128)S(1)} collective-permute-done((f32[8,128]{1,0:T(8,128)S(1)}, f32[8,128]{1,0:T(8,128)S(1)}, u32[]{:S(2)}, u32[]{:S(2)}) %collective-permute-start.2) | collective-permute-done | bytes 4128 | tf_op jit(solution)/shard_map/error/ppermute | solution.py:312
  95.3 0.3 collective-permute-done.1
  95.6 0.6 add_bitcast_fusion
Async XLA Ops:
  35.8 3.8 %collective-permute-start = (bf16[32,88,128]{2,1,0:T(8,128)(2,1)S(1)}, bf16[32,88,128]{2,1,0:T(8,128)(2,1)S(1)}, u32[]{:S(2)}, u32[]{:S(2)}) collective-permute-start(bf16[32,88,128]{2,1,0:T(8,128)(2,1)S(1)} %all_to_all.10.in_ref), channel_id=1, source_target_pairs={{0,4},{4,0},{1,5},{5,1},{2,6},{6,2},{3,7},{7,3},{8,12},{12,8},{9,1... | collective-permute-start | bytes 2162696 | tf_op jit(solution)/shard_map/to_other_core/ppermute | solution.py:340
  87.6 6.2 %collective-permute-start.3 = (f32[8,128]{1,0:T(8,128)S(1)}, f32[8,128]{1,0:T(8,128)S(1)}, u32[]{:S(2)}, u32[]{:S(2)}) collective-permute-start(f32[8,128]{1,0:T(8,128)S(1)} %error.1), channel_id=1, source_target_pairs={{0,3},{1,0},{2,1},{3,2},{4,7},{5,4},{6,5},{7,6},{8,11},{9,8},{10,9... | collective-permute-start | bytes 12296 | tf_op jit(solution)/shard_map/error/ppermute | solution.py:312
  90.5 4.8 %collective-permute-start.2 = (f32[8,128]{1,0:T(8,128)S(1)}, f32[8,128]{1,0:T(8,128)S(1)}, u32[]{:S(2)}, u32[]{:S(2)}) collective-permute-start(f32[8,128]{1,0:T(8,128)S(1)} %error.1), channel_id=1, source_target_pairs={{0,1},{1,2},{2,3},{3,0},{4,5},{5,6},{6,7},{7,4},{8,9},{9,10},{10,1... | collective-permute-start | bytes 12296 | tf_op jit(solution)/shard_map/error/ppermute | solution.py:312
  90.5 5.1 %collective-permute-start.1 = (f32[8,128]{1,0:T(8,128)S(1)}, f32[8,128]{1,0:T(8,128)S(1)}, u32[]{:S(2)}, u32[]{:S(2)}) collective-permute-start(f32[8,128]{1,0:T(8,128)S(1)} %error.1), channel_id=1, source_target_pairs={{0,2},{1,3},{2,0},{3,1},{4,6},{5,7},{6,4},{7,5},{8,10},{9,11},{10,... | collective-permute-start | bytes 12296 | tf_op jit(solution)/shard_map/error/ppermute | solution.py:312

commit v6 on v5

--- a/solution.py
+++ b/solution.py
@@ -16,6 +16,9 @@
 GROUP = 8
 
 CHIPS = 32
+Z_BITS = ("z2", "z1", "z0")
+CHIP_PLACES = ("y", "z0", "z1", "z2")
+DP = (*Z_BITS, "y", "core")
 ROWS_IN = 88
 ROWS_OUT = 24
 
@@ -72,7 +75,15 @@
         at = pl.ds(pl.multiple_of(chip * 32, 32), 32)
         books = book_rows[at, :]
         rows = [emb_rows[at, :], shared, books[0:8], books[16:24], books[8:12], books[24:28]]
-        out_ref[chip] = jnp.concatenate(rows, axis=0).astype(BF16)
+        out_ref[place_of(chip)] = jnp.concatenate(rows, axis=0).astype(BF16)
+
+
+def place_of(chip):
+    return (chip & 3) * 8 + ((chip >> 2) & 1) * 4 + ((chip >> 3) & 1) * 2 + (chip >> 4)
+
+
+def chip_in(place):
+    return (place & 1) * 16 + ((place >> 1) & 1) * 8 + ((place >> 2) & 1) * 4 + (place >> 3)
 
 
 def open_chip(rows, is_first):
@@ -144,9 +155,9 @@
     is_first = lax.axis_index("core") == 0
 
     @pl.loop(0, CHIPS, unroll=2)
-    def _(chip):
-        at = pl.ds(pl.multiple_of(chip * 8, 8), 8)
-        values, coded, weight, _ = open_chip(in_ref[chip], is_first)
+    def _(place):
+        at = pl.ds(pl.multiple_of(place * 8, 8), 8)
+        values, coded, weight, _ = open_chip(in_ref[place], is_first)
         residual[0, at, :] = values[0:8]
         residual[1, at, :] = values[8:16]
         weights[at, :] = weight
@@ -170,9 +181,9 @@
     for half, ref in enumerate((in_ref, other_ref)):
 
         @pl.loop(0, CHIPS, unroll=2)
-        def _(chip):
-            at = pl.ds(pl.multiple_of((half * CHIPS + chip) * 8, 8), 8)
-            values, coded, weight, books = open_chip(ref[chip], is_first)
+        def _(place):
+            at = pl.ds(pl.multiple_of((half * CHIPS + place) * 8, 8), 8)
+            values, coded, weight, books = open_chip(ref[place], is_first)
             residual[0, at, :] = values[0:8]
             residual[1, at, :] = values[8:16]
             weights[at, :] = weight
@@ -180,7 +191,7 @@
             for section in range(SECTIONS):
                 runs[section, at, :] = run[section * 8 : section * 8 + 8]
                 codes[section, at, :] = code[section * 8 : section * 8 + 8]
-            source = chip * 2 + (core if half == 0 else 1 - core)
+            source = chip_in(place) * 2 + (core if half == 0 else 1 - core)
             books_in[pl.ds(pl.multiple_of(source * 16, 16), 16), :] = books
 
     books_out[...] = jnp.zeros_like(books_out)
@@ -262,9 +273,9 @@
     for half in range(2):
 
         @pl.loop(0, CHIPS, unroll=8)
-        def _(chip):
-            left = take_block(SECTIONS - 1, half * CHIPS + chip)
-            source = chip * 2 + (core if half == 0 else 1 - core)
+        def _(place):
+            left = take_block(SECTIONS - 1, half * CHIPS + place)
+            source = chip_in(place) * 2 + (core if half == 0 else 1 - core)
             books = books_out[pl.ds(pl.multiple_of(source * 8, 8), 8), :]
             rows = [left[0].astype(F32), left[1].astype(F32), books]
             out_ref[source] = jnp.concatenate(rows, axis=0).astype(BF16)
@@ -335,7 +346,7 @@
             compiler_params=pltpu.CompilerParams(vmem_limit_bytes=63 * 1024 * 1024),
         )(embeddings, code_ids, item_weight.reshape(8, 128), codebooks)
     with jax.named_scope("to_features"):
-        mine = lax.all_to_all(packed, "chip", 0, 0, tiled=True)
+        mine = lax.all_to_all(packed, CHIP_PLACES, 0, 0, tiled=True)
     with jax.named_scope("to_other_core"):
         other = lax.ppermute(mine, "core", [(0, 1), (1, 0)])
     with jax.named_scope("first_sums"):
@@ -373,7 +384,7 @@
             compiler_params=params,
         )(mine, other, first)
     with jax.named_scope("to_items"):
-        back = lax.all_to_all(done, ("chip", "core"), 0, 0, tiled=True)
+        back = lax.all_to_all(done, DP, 0, 0, tiled=True)
     with jax.named_scope("error"):
         error = pl.pallas_call(
             error_kernel, out_shape=jax.ShapeDtypeStruct((8, 128), F32), compiler_params=params
@@ -396,11 +407,10 @@
 
 
 def solution(mesh):
-    dp, feat = mesh.devices.shape
-    split = Mesh(mesh.devices.reshape(dp // 2, 2, feat), ("chip", "core", "feat"))
-    dp_axes = ("chip", "core")
-    in_specs = (P(dp_axes, "feat"), P(None, dp_axes), P(None, dp_axes, "feat"), P(dp_axes))
-    out_specs = (P(None, dp_axes, "feat"), P(dp_axes, "feat"), P(dp_axes))
+    feat = mesh.devices.shape[1]
+    split = Mesh(mesh.devices.reshape(2, 2, 2, 4, 2, feat), (*DP, "feat"))
+    in_specs = (P(DP, "feat"), P(None, DP), P(None, DP, "feat"), P(DP))
+    out_specs = (P(None, DP, "feat"), P(DP, "feat"), P(DP))
     return jax.shard_map(
         per_device, mesh=split, in_specs=in_specs, out_specs=out_specs, check_vma=False
     )

time: 97.1 us -> 97.2 us (level)
  no operation moved by 1% of the time
where the time goes in v6:
time: 97.2 us; the launch traced here: 96.3 us
  blocking collectives  53.5 us (55%)
  Pallas kernels  34.7 us (36%)
  starting transfers between devices  5.12 us (5%)
  waiting for transfers between devices  1.77 us (2%)
    all_to_all x1, blocking collectives, per_device(): mine = lax.all_to_all(packed, CHIP_PLACES, 0, 0, tiled=True)  32.4 us
    pallas_call x1, Pallas kernels, per_device(): pl.pallas_call(sections_kernel, out_shape=jax.ShapeDtypeStruct((BLOCKS, R...  27.2 us
    all_to_all x1, blocking collectives, per_device(): back = lax.all_to_all(done, DP, 0, 0, tiled=True)  21 us
    ppermute x3, starting transfers between devices, sum_over_feat(): lax.ppermute(value, 'feat', [(at, (at + step) % 4) for at in range(4)])  5.12 us
    pallas_call x1, Pallas kernels, per_device(): pl.pallas_call(first_kernel, out_shape=jax.ShapeDtypeStruct((3 * RUNS, 12...  3.83 us
    pallas_call x1, Pallas kernels, per_device(): pl.pallas_call(pack_kernel, out_shape=jax.ShapeDtypeStruct((CHIPS, ROWS_I...  2.45 us
  transfers between devices with their start and end apart: 4, of which 2 were waited for; matrix products, arithmetic and copies ran while one was open for 0% of the time, Pallas kernels for 5%

profile of v6, /device:TPU:8, one launch (start us, length us, event | category | flops | bytes accessed | tf_op | source)
XLA Modules:
  0.0 96.3 jit_solution(1632608517334204392)
XLA Ops:
  0.6 2.4 %pack.1 = bf16[32,88,128]{2,1,0:T(8,128)(2,1)} custom-call(bf16[1024,128]{1,0:T(8,128)(2,1)} %emb_hbm.1, s32[3,1024]{1,0:T(4,128)} %ids_hbm.1, bf16[8,128]{1,0:T(8,128)(2,1)} %bitcast.3, f32[3,128,128]{2,1,0:T(8,128)} %book_hbm.1), custom_call_target="tpu_custom_call" | custom-call | tf_op jit(solution)/shard_map/pack/pallas_call | solution.py:332
  3.1 32.4 %all_to_all.10.in_ref = bf16[32,88,128]{2,1,0:T(8,128)(2,1)S(1)} all-to-all(bf16[32,88,128]{2,1,0:T(8,128)(2,1)} %pack.1), channel_id=1, replica_groups=mesh['z2'=2,'z1'=2,'z0'=2,'y'=4,'core'=2,'feat'=4] {'y','z0','z1','z2'}, dimensions={0} | all-to-all | bytes 1441792 | tf_op jit(solution)/shard_map/to_features/all_to_all | solution.py:349
  35.5 0.0 collective-permute-start
  35.5 3.8 %first_sums.1.first_ref = f32[192,128]{1,0:T(8,128)S(1)} custom-call(bf16[32,88,128]{2,1,0:T(8,128)(2,1)S(1)} %all_to_all.10.in_ref), custom_call_target="tpu_custom_call" | custom-call | flops 1610612736 | bytes 1048576 | tf_op jit(solution)/shard_map/first_sums/pallas_call | solution.py:353
  39.4 0.0 collective-permute-done.other_ref
  39.4 27.2 %sections.1 = bf16[64,24,128]{2,1,0:T(8,128)(2,1)S(1)} custom-call(bf16[32,88,128]{2,1,0:T(8,128)(2,1)S(1)} %all_to_all.10.in_ref, bf16[32,88,128]{2,1,0:T(8,128)(2,1)S(1)} %collective-permute-done.other_ref, f32[192,128]{1,0:T(8,128)S(1)} %first_sums.1.first_ref), custom_call_target="tpu_custom_call" | custom-call | tf_op jit(solution)/shard_map/sections/pallas_call | solution.py:368
  66.6 21.0 %all_to_all.11.in_ref = bf16[64,24,128]{2,1,0:T(8,128)(2,1)S(1)} all-to-all(bf16[64,24,128]{2,1,0:T(8,128)(2,1)S(1)} %sections.1), channel_id=1, replica_groups=mesh['z2'=2,'z1'=2,'z0'=2,'y'=4,'core'=2,'feat'=4] {'z2','z1','z0','y','..., dimensions={0} | all-to-all | bytes 786432 | tf_op jit(solution)/shard_map/to_items/all_to_all | solution.py:387
  87.6 0.2 error.1
  87.8 2.8 %collective-permute-start.3 = (f32[8,128]{1,0:T(8,128)S(1)}, f32[8,128]{1,0:T(8,128)S(1)}, u32[]{:S(2)}, u32[]{:S(2)}) collective-permute-start(f32[8,128]{1,0:T(8,128)S(1)} %error.1), channel_id=1, source_target_pairs={{0,3},{1,0},{2,1},{3,2},{4,7},{5,4},{6,5},{7,6},{8,11},{9,8},{10,9... | collective-permute-start | bytes 12296 | tf_op jit(solution)/shard_map/error/ppermute | solution.py:323
  90.6 0.0 collective-permute-start.2
  90.6 2.3 %collective-permute-start.1 = (f32[8,128]{1,0:T(8,128)S(1)}, f32[8,128]{1,0:T(8,128)S(1)}, u32[]{:S(2)}, u32[]{:S(2)}) collective-permute-start(f32[8,128]{1,0:T(8,128)S(1)} %error.1), channel_id=1, source_target_pairs={{0,2},{1,3},{2,0},{3,1},{4,6},{5,7},{6,4},{7,5},{8,10},{9,11},{10,... | collective-permute-start | bytes 12296 | tf_op jit(solution)/shard_map/error/ppermute | solution.py:323
  92.9 1.1 %unpack.1 = (f32[3,128,128]{2,1,0:T(8,128)}, bf16[1024,128]{1,0:T(8,128)(2,1)}) custom-call(bf16[64,24,128]{2,1,0:T(8,128)(2,1)S(1)} %all_to_all.11.in_ref), custom_call_target="tpu_custom_call" | custom-call | tf_op jit(solution)/shard_map/unpack/pallas_call | solution.py:394
  94.0 0.0 collective-permute-done.3
  94.0 1.5 %collective-permute-done.2 = f32[8,128]{1,0:T(8,128)S(1)} collective-permute-done((f32[8,128]{1,0:T(8,128)S(1)}, f32[8,128]{1,0:T(8,128)S(1)}, u32[]{:S(2)}, u32[]{:S(2)}) %collective-permute-start.2) | collective-permute-done | bytes 4128 | tf_op jit(solution)/shard_map/error/ppermute | solution.py:323
  95.5 0.3 collective-permute-done.1
  95.7 0.6 add_bitcast_fusion
Async XLA Ops:
  35.5 3.8 %collective-permute-start = (bf16[32,88,128]{2,1,0:T(8,128)(2,1)S(1)}, bf16[32,88,128]{2,1,0:T(8,128)(2,1)S(1)}, u32[]{:S(2)}, u32[]{:S(2)}) collective-permute-start(bf16[32,88,128]{2,1,0:T(8,128)(2,1)S(1)} %all_to_all.10.in_ref), channel_id=1, source_target_pairs={{0,4},{4,0},{1,5},{5,1},{2,6},{6,2},{3,7},{7,3},{8,12},{12,8},{9,1... | collective-permute-start | bytes 2162696 | tf_op jit(solution)/shard_map/to_other_core/ppermute | solution.py:351
  87.8 6.2 %collective-permute-start.3 = (f32[8,128]{1,0:T(8,128)S(1)}, f32[8,128]{1,0:T(8,128)S(1)}, u32[]{:S(2)}, u32[]{:S(2)}) collective-permute-start(f32[8,128]{1,0:T(8,128)S(1)} %error.1), channel_id=1, source_target_pairs={{0,3},{1,0},{2,1},{3,2},{4,7},{5,4},{6,5},{7,6},{8,11},{9,8},{10,9... | collective-permute-start | bytes 12296 | tf_op jit(solution)/shard_map/error/ppermute | solution.py:323
  90.6 4.8 %collective-permute-start.2 = (f32[8,128]{1,0:T(8,128)S(1)}, f32[8,128]{1,0:T(8,128)S(1)}, u32[]{:S(2)}, u32[]{:S(2)}) collective-permute-start(f32[8,128]{1,0:T(8,128)S(1)} %error.1), channel_id=1, source_target_pairs={{0,1},{1,2},{2,3},{3,0},{4,5},{5,6},{6,7},{7,4},{8,9},{9,10},{10,1... | collective-permute-start | bytes 12296 | tf_op jit(solution)/shard_map/error/ppermute | solution.py:323
  90.6 5.1 %collective-permute-start.1 = (f32[8,128]{1,0:T(8,128)S(1)}, f32[8,128]{1,0:T(8,128)S(1)}, u32[]{:S(2)}, u32[]{:S(2)}) collective-permute-start(f32[8,128]{1,0:T(8,128)S(1)} %error.1), channel_id=1, source_target_pairs={{0,2},{1,3},{2,0},{3,1},{4,6},{5,7},{6,4},{7,5},{8,10},{9,11},{10,... | collective-permute-start | bytes 12296 | tf_op jit(solution)/shard_map/error/ppermute | solution.py:323

commit v7 on v5

--- a/solution.py
+++ b/solution.py
@@ -67,7 +67,7 @@
 
     shared = shared_rows[...]
 
-    @pl.loop(0, CHIPS, unroll=4)
+    @pl.loop(0, CHIPS, unroll=8)
     def _(chip):
         at = pl.ds(pl.multiple_of(chip * 32, 32), 32)
         books = book_rows[at, :]
@@ -143,7 +143,7 @@
 def first_kernel(in_ref, total, runs, codes, weights, residual):
     is_first = lax.axis_index("core") == 0
 
-    @pl.loop(0, CHIPS, unroll=2)
+    @pl.loop(0, CHIPS, unroll=8)
     def _(chip):
         at = pl.ds(pl.multiple_of(chip * 8, 8), 8)
         values, coded, weight, _ = open_chip(in_ref[chip], is_first)
@@ -169,7 +169,7 @@
 
     for half, ref in enumerate((in_ref, other_ref)):
 
-        @pl.loop(0, CHIPS, unroll=2)
+        @pl.loop(0, CHIPS, unroll=8)
         def _(chip):
             at = pl.ds(pl.multiple_of((half * CHIPS + chip) * 8, 8), 8)
             values, coded, weight, books = open_chip(ref[chip], is_first)
@@ -307,12 +307,18 @@
         book_ref[section] = turned.T
 
 
-def sum_over_feat(value):
+def sum_kernel(value_ref, one_ref, two_ref, three_ref, out_ref):
+    out_ref[...] = (value_ref[...] + two_ref[...]) + (one_ref[...] + three_ref[...])
+
+
+def sum_over_feat(value, params):
     one, two, three = [
         lax.ppermute(value, "feat", [(at, (at + step) % 4) for at in range(4)])
         for step in range(1, 4)
     ]
-    return (value + two) + (one + three)
+    return pl.pallas_call(
+        sum_kernel, out_shape=jax.ShapeDtypeStruct(value.shape, F32), compiler_params=params
+    )(value, one, two, three)
 
 
 def per_device(embeddings, code_ids, codebooks, item_weight):
@@ -378,7 +384,7 @@
         error = pl.pallas_call(
             error_kernel, out_shape=jax.ShapeDtypeStruct((8, 128), F32), compiler_params=params
         )(back)
-        item_error = sum_over_feat(error).reshape(1024)
+        item_error = sum_over_feat(error, params).reshape(1024)
     with jax.named_scope("unpack"):
         updated, left = pl.pallas_call(
             unpack_kernel,

time: 97.1 us -> 96.7 us (level)
  waiting for transfers between devices: 1.76 us -> 2.88 us
    ppermute x3, waiting for transfers between devices: 1.76 us -> 2.88 us  [sum_over_feat(): lax.ppermute(value, 'feat', [(at, (at + step) % 4) for at in range(4)])]
where the time goes in v7:
time: 96.7 us; the launch traced here: 96.5 us
  blocking collectives  53.4 us (55%)
  Pallas kernels  35 us (36%)
  starting transfers between devices  4.52 us (5%)
  waiting for transfers between devices  2.88 us (3%)
    all_to_all x1, blocking collectives, per_device(): mine = lax.all_to_all(packed, 'chip', 0, 0, tiled=True)  32.8 us
    pallas_call x1, Pallas kernels, per_device(): pl.pallas_call(sections_kernel, out_shape=jax.ShapeDtypeStruct((BLOCKS, R...  27.1 us
    all_to_all x1, blocking collectives, per_device(): back = lax.all_to_all(done, ('chip', 'core'), 0, 0, tiled=True)  20.6 us
    ppermute x3, starting transfers between devices, sum_over_feat(): lax.ppermute(value, 'feat', [(at, (at + step) % 4) for at in range(4)])  4.52 us
    pallas_call x1, Pallas kernels, per_device(): pl.pallas_call(first_kernel, out_shape=jax.ShapeDtypeStruct((3 * RUNS, 12...  3.75 us
    ppermute x3, waiting for transfers between devices, sum_over_feat(): lax.ppermute(value, 'feat', [(at, (at + step) % 4) for at in range(4)])  2.88 us
    pallas_call x1, Pallas kernels, per_device(): pl.pallas_call(pack_kernel, out_shape=jax.ShapeDtypeStruct((CHIPS, ROWS_I...  2.34 us
  transfers between devices with their start and end apart: 4, of which 2 were waited for; matrix products, arithmetic and copies ran while one was open for 0% of the time, Pallas kernels for 5%

profile of v7, /device:TPU:8, one launch (start us, length us, event | category | flops | bytes accessed | tf_op | source)
XLA Modules:
  0.0 96.5 jit_solution(18220319797464347872)
XLA Ops:
  0.6 2.3 %pack.1 = bf16[32,88,128]{2,1,0:T(8,128)(2,1)} custom-call(bf16[1024,128]{1,0:T(8,128)(2,1)} %emb_hbm.1, s32[3,1024]{1,0:T(4,128)} %ids_hbm.1, bf16[8,128]{1,0:T(8,128)(2,1)} %bitcast.3, f32[3,128,128]{2,1,0:T(8,128)} %book_hbm.1), custom_call_target="tpu_custom_call" | custom-call | tf_op jit(solution)/shard_map/pack/pallas_call | solution.py:327
  3.0 32.8 %all_to_all.10.in_ref = bf16[32,88,128]{2,1,0:T(8,128)(2,1)S(1)} all-to-all(bf16[32,88,128]{2,1,0:T(8,128)(2,1)} %pack.1), channel_id=1, replica_groups=mesh['chip'=32,'core'=2,'feat'=4] {'chip'}, dimensions={0} | all-to-all | bytes 1441792 | tf_op jit(solution)/shard_map/to_features/all_to_all | solution.py:344
  35.7 0.0 collective-permute-start
  35.7 3.8 %first_sums.1.first_ref = f32[192,128]{1,0:T(8,128)S(1)} custom-call(bf16[32,88,128]{2,1,0:T(8,128)(2,1)S(1)} %all_to_all.10.in_ref), custom_call_target="tpu_custom_call" | custom-call | flops 1610612736 | bytes 1048576 | tf_op jit(solution)/shard_map/first_sums/pallas_call | solution.py:348
  39.5 0.0 collective-permute-done.other_ref
  39.5 27.1 %sections.1 = bf16[64,24,128]{2,1,0:T(8,128)(2,1)S(1)} custom-call(bf16[32,88,128]{2,1,0:T(8,128)(2,1)S(1)} %all_to_all.10.in_ref, bf16[32,88,128]{2,1,0:T(8,128)(2,1)S(1)} %collective-permute-done.other_ref, f32[192,128]{1,0:T(8,128)S(1)} %first_sums.1.first_ref), custom_call_target="tpu_custom_call" | custom-call | tf_op jit(solution)/shard_map/sections/pallas_call | solution.py:363
  66.6 20.6 %all_to_all.11.in_ref = bf16[64,24,128]{2,1,0:T(8,128)(2,1)S(1)} all-to-all(bf16[64,24,128]{2,1,0:T(8,128)(2,1)S(1)} %sections.1), channel_id=1, replica_groups=mesh['chip'=32,'core'=2,'feat'=4] {'chip','core'}, dimensions={0} | all-to-all | bytes 786432 | tf_op jit(solution)/shard_map/to_items/all_to_all | solution.py:382
  87.2 0.2 error.2.value_ref
  87.4 2.8 %collective-permute-start.3 = (f32[8,128]{1,0:T(8,128)S(1)}, f32[8,128]{1,0:T(8,128)S(1)}, u32[]{:S(2)}, u32[]{:S(2)}) collective-permute-start(f32[8,128]{1,0:T(8,128)S(1)} %error.2.value_ref), channel_id=1, source_target_pairs={{0,3},{1,0},{2,1},{3,2},{4,7},{5,4},{6,5},{7,6},{8,11},{9,8},{10,9... | collective-permute-start | bytes 12296 | tf_op jit(solution)/shard_map/error/ppermute | solution.py:316
  90.2 0.8 collective-permute-start.2
  91.0 0.9 collective-permute-start.1
  91.9 1.1 %unpack.1 = (f32[3,128,128]{2,1,0:T(8,128)}, bf16[1024,128]{1,0:T(8,128)(2,1)}) custom-call(bf16[64,24,128]{2,1,0:T(8,128)(2,1)S(1)} %all_to_all.11.in_ref), custom_call_target="tpu_custom_call" | custom-call | tf_op jit(solution)/shard_map/unpack/pallas_call | solution.py:389
  93.0 0.0 collective-permute-done.3.three_ref
  93.0 2.4 %collective-permute-done.2.two_ref = f32[8,128]{1,0:T(8,128)S(1)} collective-permute-done((f32[8,128]{1,0:T(8,128)S(1)}, f32[8,128]{1,0:T(8,128)S(1)}, u32[]{:S(2)}, u32[]{:S(2)}) %collective-permute-start.2) | collective-permute-done | bytes 4128 | tf_op jit(solution)/shard_map/error/ppermute | solution.py:316
  95.4 0.5 collective-permute-done.1.one_ref
  95.9 0.6 error.3
Async XLA Ops:
  35.7 3.8 %collective-permute-start = (bf16[32,88,128]{2,1,0:T(8,128)(2,1)S(1)}, bf16[32,88,128]{2,1,0:T(8,128)(2,1)S(1)}, u32[]{:S(2)}, u32[]{:S(2)}) collective-permute-start(bf16[32,88,128]{2,1,0:T(8,128)(2,1)S(1)} %all_to_all.10.in_ref), channel_id=1, source_target_pairs={{0,4},{4,0},{1,5},{5,1},{2,6},{6,2},{3,7},{7,3},{8,12},{12,8},{9,1... | collective-permute-start | bytes 2162696 | tf_op jit(solution)/shard_map/to_other_core/ppermute | solution.py:346
  87.4 5.6 %collective-permute-start.3 = (f32[8,128]{1,0:T(8,128)S(1)}, f32[8,128]{1,0:T(8,128)S(1)}, u32[]{:S(2)}, u32[]{:S(2)}) collective-permute-start(f32[8,128]{1,0:T(8,128)S(1)} %error.2.value_ref), channel_id=1, source_target_pairs={{0,3},{1,0},{2,1},{3,2},{4,7},{5,4},{6,5},{7,6},{8,11},{9,8},{10,9... | collective-permute-start | bytes 12296 | tf_op jit(solution)/shard_map/error/ppermute | solution.py:316
  90.2 5.1 %collective-permute-start.2 = (f32[8,128]{1,0:T(8,128)S(1)}, f32[8,128]{1,0:T(8,128)S(1)}, u32[]{:S(2)}, u32[]{:S(2)}) collective-permute-start(f32[8,128]{1,0:T(8,128)S(1)} %error.2.value_ref), channel_id=1, source_target_pairs={{0,2},{1,3},{2,0},{3,1},{4,6},{5,7},{6,4},{7,5},{8,10},{9,11},{10,... | collective-permute-start | bytes 12296 | tf_op jit(solution)/shard_map/error/ppermute | solution.py:316
  91.0 4.8 %collective-permute-start.1 = (f32[8,128]{1,0:T(8,128)S(1)}, f32[8,128]{1,0:T(8,128)S(1)}, u32[]{:S(2)}, u32[]{:S(2)}) collective-permute-start(f32[8,128]{1,0:T(8,128)S(1)} %error.2.value_ref), channel_id=1, source_target_pairs={{0,1},{1,2},{2,3},{3,0},{4,5},{5,6},{6,7},{7,4},{8,9},{9,10},{10,1... | collective-permute-start | bytes 12296 | tf_op jit(solution)/shard_map/error/ppermute | solution.py:316

commit v8 on v7

--- a/solution.py
+++ b/solution.py
@@ -13,7 +13,7 @@
 BLOCKS = 64
 FEATS = 128
 prior_weight = 4.0
-GROUP = 8
+GROUP = 16
 
 CHIPS = 32
 ROWS_IN = 88

time: 96.7 us -> 96.7 us (level)
  no operation moved by 1% of the time
where the time goes in v8:
time: 96.7 us; the launch traced here: 96.4 us
  blocking collectives  53.4 us (55%)
  Pallas kernels  35 us (36%)
  starting transfers between devices  4.52 us (5%)
  waiting for transfers between devices  2.88 us (3%)
    all_to_all x1, blocking collectives, per_device(): mine = lax.all_to_all(packed, 'chip', 0, 0, tiled=True)  32.8 us
    pallas_call x1, Pallas kernels, per_device(): pl.pallas_call(sections_kernel, out_shape=jax.ShapeDtypeStruct((BLOCKS, R...  27 us
    all_to_all x1, blocking collectives, per_device(): back = lax.all_to_all(done, ('chip', 'core'), 0, 0, tiled=True)  20.6 us
    ppermute x3, starting transfers between devices, sum_over_feat(): lax.ppermute(value, 'feat', [(at, (at + step) % 4) for at in range(4)])  4.52 us
    pallas_call x1, Pallas kernels, per_device(): pl.pallas_call(first_kernel, out_shape=jax.ShapeDtypeStruct((3 * RUNS, 12...  3.75 us
    ppermute x3, waiting for transfers between devices, sum_over_feat(): lax.ppermute(value, 'feat', [(at, (at + step) % 4) for at in range(4)])  2.88 us
    pallas_call x1, Pallas kernels, per_device(): pl.pallas_call(pack_kernel, out_shape=jax.ShapeDtypeStruct((CHIPS, ROWS_I...  2.34 us
  transfers between devices with their start and end apart: 4, of which 2 were waited for; matrix products, arithmetic and copies ran while one was open for 0% of the time, Pallas kernels for 5%

profile of v8, /device:TPU:8, one launch (start us, length us, event | category | flops | bytes accessed | tf_op | source)
XLA Modules:
  0.0 96.4 jit_solution(1143943218700655143)
XLA Ops:
  0.6 2.3 %pack.1 = bf16[32,88,128]{2,1,0:T(8,128)(2,1)} custom-call(bf16[1024,128]{1,0:T(8,128)(2,1)} %emb_hbm.1, s32[3,1024]{1,0:T(4,128)} %ids_hbm.1, bf16[8,128]{1,0:T(8,128)(2,1)} %bitcast.3, f32[3,128,128]{2,1,0:T(8,128)} %book_hbm.1), custom_call_target="tpu_custom_call" | custom-call | tf_op jit(solution)/shard_map/pack/pallas_call | solution.py:327
  3.0 32.8 %all_to_all.10.in_ref = bf16[32,88,128]{2,1,0:T(8,128)(2,1)S(1)} all-to-all(bf16[32,88,128]{2,1,0:T(8,128)(2,1)} %pack.1), channel_id=1, replica_groups=mesh['chip'=32,'core'=2,'feat'=4] {'chip'}, dimensions={0} | all-to-all | bytes 1441792 | tf_op jit(solution)/shard_map/to_features/all_to_all | solution.py:344
  35.7 0.0 collective-permute-start
  35.7 3.8 %first_sums.1.first_ref = f32[192,128]{1,0:T(8,128)S(1)} custom-call(bf16[32,88,128]{2,1,0:T(8,128)(2,1)S(1)} %all_to_all.10.in_ref), custom_call_target="tpu_custom_call" | custom-call | flops 1610612736 | bytes 1048576 | tf_op jit(solution)/shard_map/first_sums/pallas_call | solution.py:348
  39.5 0.0 collective-permute-done.other_ref
  39.5 27.0 %sections.1 = bf16[64,24,128]{2,1,0:T(8,128)(2,1)S(1)} custom-call(bf16[32,88,128]{2,1,0:T(8,128)(2,1)S(1)} %all_to_all.10.in_ref, bf16[32,88,128]{2,1,0:T(8,128)(2,1)S(1)} %collective-permute-done.other_ref, f32[192,128]{1,0:T(8,128)S(1)} %first_sums.1.first_ref), custom_call_target="tpu_custom_call" | custom-call | tf_op jit(solution)/shard_map/sections/pallas_call | solution.py:363
  66.6 20.6 %all_to_all.11.in_ref = bf16[64,24,128]{2,1,0:T(8,128)(2,1)S(1)} all-to-all(bf16[64,24,128]{2,1,0:T(8,128)(2,1)S(1)} %sections.1), channel_id=1, replica_groups=mesh['chip'=32,'core'=2,'feat'=4] {'chip','core'}, dimensions={0} | all-to-all | bytes 786432 | tf_op jit(solution)/shard_map/to_items/all_to_all | solution.py:382
  87.2 0.2 error.2.value_ref
  87.3 2.8 %collective-permute-start.3 = (f32[8,128]{1,0:T(8,128)S(1)}, f32[8,128]{1,0:T(8,128)S(1)}, u32[]{:S(2)}, u32[]{:S(2)}) collective-permute-start(f32[8,128]{1,0:T(8,128)S(1)} %error.2.value_ref), channel_id=1, source_target_pairs={{0,3},{1,0},{2,1},{3,2},{4,7},{5,4},{6,5},{7,6},{8,11},{9,8},{10,9... | collective-permute-start | bytes 12296 | tf_op jit(solution)/shard_map/error/ppermute | solution.py:316
  90.2 0.8 collective-permute-start.2
  91.0 0.9 collective-permute-start.1
  91.9 1.1 %unpack.1 = (f32[3,128,128]{2,1,0:T(8,128)}, bf16[1024,128]{1,0:T(8,128)(2,1)}) custom-call(bf16[64,24,128]{2,1,0:T(8,128)(2,1)S(1)} %all_to_all.11.in_ref), custom_call_target="tpu_custom_call" | custom-call | tf_op jit(solution)/shard_map/unpack/pallas_call | solution.py:389
  92.9 0.0 collective-permute-done.3.three_ref
  92.9 2.4 %collective-permute-done.2.two_ref = f32[8,128]{1,0:T(8,128)S(1)} collective-permute-done((f32[8,128]{1,0:T(8,128)S(1)}, f32[8,128]{1,0:T(8,128)S(1)}, u32[]{:S(2)}, u32[]{:S(2)}) %collective-permute-start.2) | collective-permute-done | bytes 4128 | tf_op jit(solution)/shard_map/error/ppermute | solution.py:316
  95.3 0.5 collective-permute-done.1.one_ref
  95.8 0.6 error.3
Async XLA Ops:
  35.7 3.8 %collective-permute-start = (bf16[32,88,128]{2,1,0:T(8,128)(2,1)S(1)}, bf16[32,88,128]{2,1,0:T(8,128)(2,1)S(1)}, u32[]{:S(2)}, u32[]{:S(2)}) collective-permute-start(bf16[32,88,128]{2,1,0:T(8,128)(2,1)S(1)} %all_to_all.10.in_ref), channel_id=1, source_target_pairs={{0,4},{4,0},{1,5},{5,1},{2,6},{6,2},{3,7},{7,3},{8,12},{12,8},{9,1... | collective-permute-start | bytes 2162696 | tf_op jit(solution)/shard_map/to_other_core/ppermute | solution.py:346
  87.3 5.6 %collective-permute-start.3 = (f32[8,128]{1,0:T(8,128)S(1)}, f32[8,128]{1,0:T(8,128)S(1)}, u32[]{:S(2)}, u32[]{:S(2)}) collective-permute-start(f32[8,128]{1,0:T(8,128)S(1)} %error.2.value_ref), channel_id=1, source_target_pairs={{0,3},{1,0},{2,1},{3,2},{4,7},{5,4},{6,5},{7,6},{8,11},{9,8},{10,9... | collective-permute-start | bytes 12296 | tf_op jit(solution)/shard_map/error/ppermute | solution.py:316
  90.2 5.1 %collective-permute-start.2 = (f32[8,128]{1,0:T(8,128)S(1)}, f32[8,128]{1,0:T(8,128)S(1)}, u32[]{:S(2)}, u32[]{:S(2)}) collective-permute-start(f32[8,128]{1,0:T(8,128)S(1)} %error.2.value_ref), channel_id=1, source_target_pairs={{0,2},{1,3},{2,0},{3,1},{4,6},{5,7},{6,4},{7,5},{8,10},{9,11},{10,... | collective-permute-start | bytes 12296 | tf_op jit(solution)/shard_map/error/ppermute | solution.py:316
  91.0 4.8 %collective-permute-start.1 = (f32[8,128]{1,0:T(8,128)S(1)}, f32[8,128]{1,0:T(8,128)S(1)}, u32[]{:S(2)}, u32[]{:S(2)}) collective-permute-start(f32[8,128]{1,0:T(8,128)S(1)} %error.2.value_ref), channel_id=1, source_target_pairs={{0,1},{1,2},{2,3},{3,0},{4,5},{5,6},{6,7},{7,4},{8,9},{9,10},{10,1... | collective-permute-start | bytes 12296 | tf_op jit(solution)/shard_map/error/ppermute | solution.py:316

commit v9 on v8

--- a/solution.py
+++ b/solution.py
@@ -307,20 +307,6 @@
         book_ref[section] = turned.T
 
 
-def sum_kernel(value_ref, one_ref, two_ref, three_ref, out_ref):
-    out_ref[...] = (value_ref[...] + two_ref[...]) + (one_ref[...] + three_ref[...])
-
-
-def sum_over_feat(value, params):
-    one, two, three = [
-        lax.ppermute(value, "feat", [(at, (at + step) % 4) for at in range(4)])
-        for step in range(1, 4)
-    ]
-    return pl.pallas_call(
-        sum_kernel, out_shape=jax.ShapeDtypeStruct(value.shape, F32), compiler_params=params
-    )(value, one, two, three)
-
-
 def per_device(embeddings, code_ids, codebooks, item_weight):
     params = pltpu.CompilerParams(vmem_limit_bytes=48 * 1024 * 1024)
     with jax.named_scope("pack"):
@@ -384,7 +370,7 @@
         error = pl.pallas_call(
             error_kernel, out_shape=jax.ShapeDtypeStruct((8, 128), F32), compiler_params=params
         )(back)
-        item_error = sum_over_feat(error, params).reshape(1024)
+        item_error = lax.psum(error, "feat").reshape(1024)
     with jax.named_scope("unpack"):
         updated, left = pl.pallas_call(
             unpack_kernel,

time: 96.7 us -> 99.7 us (1.031)
  blocking collectives: 53.4 us -> 64.5 us
  starting transfers between devices: 4.52 us -> 0.01 us
  waiting for transfers between devices: 2.88 us -> 0.01 us
    psum x0 -> x1, blocking collectives: none -> 11.1 us  [per_device(): item_error = lax.psum(error, 'feat').reshape(1024)]
    ppermute x3 -> x0, starting transfers between devices: 4.52 us -> none  [sum_over_feat(): lax.ppermute(value, 'feat', [(at, (at + step) % 4) for at in range(4)])]
    ppermute x3 -> x0, waiting for transfers between devices: 2.88 us -> none  [sum_over_feat(): lax.ppermute(value, 'feat', [(at, (at + step) % 4) for at in range(4)])]
  transfers between devices with their start and end apart: 4 -> 1, of which waited for: 2 -> 0; matrix products, arithmetic and copies ran while one was open for 0% -> 0% of each run, Pallas kernels for 5% -> 4%
where the time goes in v9:
time: 99.7 us; the launch traced here: 99.5 us
  blocking collectives  64.5 us (65%)
  Pallas kernels  34.3 us (34%)
    all_to_all x1, blocking collectives, per_device(): mine = lax.all_to_all(packed, 'chip', 0, 0, tiled=True)  32.8 us
    pallas_call x1, Pallas kernels, per_device(): pl.pallas_call(sections_kernel, out_shape=jax.ShapeDtypeStruct((BLOCKS, R...  27 us
    all_to_all x1, blocking collectives, per_device(): back = lax.all_to_all(done, ('chip', 'core'), 0, 0, tiled=True)  20.6 us
    psum x1, blocking collectives, per_device(): item_error = lax.psum(error, 'feat').reshape(1024)  11.1 us
    pallas_call x1, Pallas kernels, per_device(): pl.pallas_call(first_kernel, out_shape=jax.ShapeDtypeStruct((3 * RUNS, 12...  3.75 us
    pallas_call x1, Pallas kernels, per_device(): pl.pallas_call(pack_kernel, out_shape=jax.ShapeDtypeStruct((CHIPS, ROWS_I...  2.33 us
  transfers between devices with their start and end apart: 1, of which 0 were waited for; matrix products, arithmetic and copies ran while one was open for 0% of the time, Pallas kernels for 4%

profile of v9, /device:TPU:8, one launch (start us, length us, event | category | flops | bytes accessed | tf_op | source)
XLA Modules:
  0.0 99.5 jit_solution(12419356725397067570)
XLA Ops:
  0.6 2.3 %pack.1 = bf16[32,88,128]{2,1,0:T(8,128)(2,1)} custom-call(bf16[1024,128]{1,0:T(8,128)(2,1)} %emb_hbm.1, s32[3,1024]{1,0:T(4,128)} %ids_hbm.1, bf16[8,128]{1,0:T(8,128)(2,1)} %bitcast.3, f32[3,128,128]{2,1,0:T(8,128)} %book_hbm.1), custom_call_target="tpu_custom_call" | custom-call | tf_op jit(solution)/shard_map/pack/pallas_call | solution.py:313
  3.0 32.8 %all_to_all.10.in_ref = bf16[32,88,128]{2,1,0:T(8,128)(2,1)S(1)} all-to-all(bf16[32,88,128]{2,1,0:T(8,128)(2,1)} %pack.1), channel_id=1, replica_groups=mesh['chip'=32,'core'=2,'feat'=4] {'chip'}, dimensions={0} | all-to-all | bytes 1441792 | tf_op jit(solution)/shard_map/to_features/all_to_all | solution.py:330
  35.7 0.0 collective-permute-start
  35.7 3.8 %first_sums.1.first_ref = f32[192,128]{1,0:T(8,128)S(1)} custom-call(bf16[32,88,128]{2,1,0:T(8,128)(2,1)S(1)} %all_to_all.10.in_ref), custom_call_target="tpu_custom_call" | custom-call | flops 1610612736 | bytes 1048576 | tf_op jit(solution)/shard_map/first_sums/pallas_call | solution.py:334
  39.5 0.0 collective-permute-done.other_ref
  39.5 27.0 %sections.1 = bf16[64,24,128]{2,1,0:T(8,128)(2,1)S(1)} custom-call(bf16[32,88,128]{2,1,0:T(8,128)(2,1)S(1)} %all_to_all.10.in_ref, bf16[32,88,128]{2,1,0:T(8,128)(2,1)S(1)} %collective-permute-done.other_ref, f32[192,128]{1,0:T(8,128)S(1)} %first_sums.1.first_ref), custom_call_target="tpu_custom_call" | custom-call | tf_op jit(solution)/shard_map/sections/pallas_call | solution.py:349
  66.5 20.6 %all_to_all.11.in_ref = bf16[64,24,128]{2,1,0:T(8,128)(2,1)S(1)} all-to-all(bf16[64,24,128]{2,1,0:T(8,128)(2,1)S(1)} %sections.1), channel_id=1, replica_groups=mesh['chip'=32,'core'=2,'feat'=4] {'chip','core'}, dimensions={0} | all-to-all | bytes 786432 | tf_op jit(solution)/shard_map/to_items/all_to_all | solution.py:368
  87.2 0.2 error.1
  87.3 11.1 %psum.7 = f32[1024]{0:T(1024)} all-reduce(f32[1024]{0:T(1024)S(1)} %bitcast.2), channel_id=1, replica_groups=mesh['chip'=32,'core'=2,'feat'=4] {'feat'}, use_global_device_ids=true, to_apply=%region_0.0 | all-reduce | flops 1024 | bytes 8192 | tf_op jit(solution)/shard_map/error/psum | solution.py:373
  98.4 1.1 %unpack.1 = (f32[3,128,128]{2,1,0:T(8,128)}, bf16[1024,128]{1,0:T(8,128)(2,1)}) custom-call(bf16[64,24,128]{2,1,0:T(8,128)(2,1)S(1)} %all_to_all.11.in_ref), custom_call_target="tpu_custom_call" | custom-call | tf_op jit(solution)/shard_map/unpack/pallas_call | solution.py:375
Async XLA Ops:
  35.7 3.8 %collective-permute-start = (bf16[32,88,128]{2,1,0:T(8,128)(2,1)S(1)}, bf16[32,88,128]{2,1,0:T(8,128)(2,1)S(1)}, u32[]{:S(2)}, u32[]{:S(2)}) collective-permute-start(bf16[32,88,128]{2,1,0:T(8,128)(2,1)S(1)} %all_to_all.10.in_ref), channel_id=1, source_target_pairs={{0,4},{4,0},{1,5},{5,1},{2,6},{6,2},{3,7},{7,3},{8,12},{12,8},{9,1... | collective-permute-start | bytes 2162696 | tf_op jit(solution)/shard_map/to_other_core/ppermute | solution.py:332
